TPU v7x, 32 devices: a whole 2x2x4 slice. The times are simulated.
32 devices in a mesh: rep: 4 (over z), exp: 8 (over y, x, core).
Axes of the slice: x: 2, y: 2, z: 4, core: 2. Of those that a mesh axis runs over, the one named last changes fastest.
Arguments:
- tokens: bfloat16 [512, 4096], P(('rep', 'exp')), may hold values from -6 to 6
- routed_experts: int32 [512, 8], P(('rep', 'exp')), may hold values from 0 to 15, all different within a row; in each aligned block of 16 rows (0 to 15, 16 to 31, ...) at most 12 rows name the same one
- route_weights: float32 [512, 8], P(('rep', 'exp')), may hold values from 0.02 to 0.5
- gate_weight: bfloat16 [16, 1536, 4096], P('exp', 'rep'), may hold values from -0.09375 to 0.09375
- up_weight: bfloat16 [16, 1536, 4096], P('exp', 'rep'), may hold values from -0.09375 to 0.09375
- down_weight: bfloat16 [16, 1536, 4096], P('exp', 'rep'), may hold values from -0.15625 to 0.15625
Outputs:
- layer_output: bfloat16 [512, 4096], P(('rep', 'exp'))
Inputs may be any that keep to these rules, and one draw needn't show every extreme that they name: `routed_experts`: each token names 8 different experts. Among the 16 tokens of one device (aligned blocks of rows), no expert is named more than 12 times, a bound that some block reaches.
All inputs are finite; a program needn't handle non-finite values.
Results may differ from a plain program's by a relative error of at most 0.01.
Values may be sent and summed in bfloat16 or wider, within the bound.
No kernel may reach another device: no remote copies, remote signals or barrier semaphores. Data moves between devices by JAX's collectives and lax.ppermute only.
A program may use at most 128 MiB of HBM per device.

v0:
```python
import jax
import jax.numpy as jnp
from jax import lax
from jax.sharding import PartitionSpec as P


def slot_table(experts, expert_count, capacity):
    blocks = experts.shape[0]
    flattened = experts.reshape(blocks, -1)
    onehot = (
        flattened[:, :, None] == jnp.arange(expert_count, dtype=jnp.int32)[None, None, :]
    ).astype(jnp.int32)
    before = jnp.cumsum(onehot, axis=1) - onehot
    position = jnp.sum(before * onehot, axis=2)
    return flattened * capacity + position


def token_picks(slots, top_count, slot_count):
    blocks = slots.shape[0]
    grouped = slots.reshape(blocks, 1, -1, top_count)
    return jnp.any(grouped == jnp.arange(slot_count, dtype=jnp.int32)[None, :, None, None], axis=3)


def routing_column(route_weights, routed_experts):
    as_float = routed_experts.astype(jnp.float32)
    weights_all, experts_all = (
        lax.all_gather(route_weights, "rep", axis=0, tiled=True),
        lax.all_gather(as_float, "rep", axis=0, tiled=True),
    )
    return (weights_all, experts_all.astype(jnp.int32))


def on_device(tokens, routed_experts, route_weights, gate_weight, up_weight, down_weight):
    replicas = lax.axis_size("rep")
    owners = lax.axis_size("exp")
    token_rows, model_width = tokens.shape
    top_count = routed_experts.shape[1]
    local_experts = gate_weight.shape[0]
    expert_count = local_experts * owners
    capacity = max(2, 3 * token_rows * top_count // (2 * expert_count))
    slot_count = expert_count * capacity
    own_slots = slot_table(routed_experts[None], expert_count, capacity)
    column = None
    column_slots = None
    selected = token_picks(own_slots, top_count, slot_count)[0].astype(jnp.bfloat16)
    buffer = jnp.dot(selected, tokens, preferred_element_type=jnp.float32).astype(jnp.bfloat16)
    buffer = buffer.reshape(owners, local_experts, capacity, model_width)
    arrived = lax.all_to_all(buffer, "exp", split_axis=0, concat_axis=2, tiled=True)
    rows_now = lax.all_gather(arrived, "rep", axis=2, tiled=True)[0]
    gate_value = jnp.einsum(
        "emd,efd->emf", rows_now, gate_weight, preferred_element_type=jnp.float32
    )
    up_value = jnp.einsum("emd,efd->emf", rows_now, up_weight, preferred_element_type=jnp.float32)
    hidden = (jax.nn.silu(gate_value) * up_value).astype(jnp.bfloat16)
    outcome = jnp.einsum("emf,efd->emd", hidden, down_weight, preferred_element_type=jnp.float32)
    outcome = lax.optimization_barrier(outcome.astype(jnp.bfloat16))
    outcomes = outcome[None]
    outcomes = outcomes.reshape(local_experts, replicas, owners, capacity, model_width)
    column = routing_column(route_weights, routed_experts)
    column_slots = slot_table(
        column[1].reshape(replicas, token_rows, top_count), expert_count, capacity
    )
    returned = lax.all_to_all(outcomes, "exp", split_axis=2, concat_axis=0, tiled=True)
    returned = returned.reshape(expert_count, replicas, capacity, model_width)
    expert_index = column_slots // capacity
    place_index = column_slots % capacity
    replica_index = jnp.broadcast_to(
        jnp.arange(replicas, dtype=jnp.int32)[:, None], column_slots.shape
    )
    picked = returned[expert_index, replica_index, place_index].astype(jnp.float32)
    column_weights = column[0].reshape(replicas, token_rows, top_count)
    weighted = jnp.sum(
        picked.reshape(replicas, token_rows, top_count, model_width)
        * column_weights[:, :, :, None],
        axis=2,
    )
    summed = lax.psum_scatter(weighted, "rep", scatter_dimension=0, tiled=True)
    return summed.reshape(token_rows, model_width).astype(jnp.bfloat16)


def solution(mesh):
    placed = (
        P(("rep", "exp"), None),
        P(("rep", "exp"), None),
        P(("rep", "exp"), None),
        P("exp", "rep", None),
        P("exp", "rep", None),
        P("exp", "rep", None),
    )
    return jax.shard_map(
        on_device, mesh=mesh, in_specs=placed, out_specs=P(("rep", "exp"), None), check_vma=False
    )
```

profile of v0, /device:TPU:0, one launch (start us, length us, event | category | flops | bytes accessed | tf_op | source)
XLA Modules:
  0.0 335.7 jit_solution(136606165095649366)
XLA Ops:
  6.5 0.8 copy.31
  7.3 0.1 eq.65
  7.4 0.1 fusion.16
  7.5 0.2 reduce_window_sum.22
  7.7 0.2 select_reduce_fusion.1
  7.9 0.1 reduce_sum.32
  8.0 0.1 fusion.15
  8.1 1.8 convolution_convert_fusion.1
  9.9 2.3 reshape.225
  12.2 1.6 copy.33
  13.9 25.9 %all_to_all.33 = bf16[8,2,12,4096]{3,1,2,0:T(2,128)(2,1)S(1)} all-to-all(bf16[8,2,12,4096]{3,1,2,0:T(2,128)(2,1)S(1)} %copy.33), channel_id=1, replica_groups=mesh['rep'=4,'exp'=8] {'exp'}, dimensions={0} | all-to-all | bytes 3145728 | tf_op jit(solution)/shard_map/all_to_all | solution.py:48
  39.8 2.0 copy.34
  41.8 114.9 %all-gather.4.cloned.1.call-done = bf16[1,2,384,4096]{3,2,1,0:T(8,128)(2,1)} async-done(((bf16[1,2,96,4096]{3,2,1,0:T(8,128)(2,1)}), bf16[1,2,384,4096]{3,2,1,0:T(8,128)(2,1)}) %all-gather.4.cloned.1.call-update) | async-done | bytes 6291472 | tf_op jit(solution)/shard_map/all_gather | solution.py:49
  156.7 8.1 %fusion.3 = f32[2,384,384]{2,1,0:T(8,128)S(1)} fusion(bf16[2,384,4096]{2,1,0:T(8,128)(2,1)} %param.9, bf16[1,2,384,4096]{3,2,1,0:T(8,128)(2,1)} %all-gather.4.cloned.1.call-done), kind=kOutput, calls=%fused_computation.6 | convolution fusion | flops 2415919104 | bytes 13762560 | tf_op jit(solution)/shard_map/emd,efd->emf/dot_general | solution.py:50
  164.8 12.4 %convolution_convert_fusion = bf16[2,384,4096]{2,1,0:T(8,128)(2,1)} fusion(bf16[2,384,4096]{2,1,0:T(8,128)(2,1)} %param.11, bf16[2,384,4096]{2,1,0:T(8,128)(2,1)} %param.10, bf16[1,2,384,4096]{3,2,1,0:T(8,128)(2,1)} %all-gather.4.cloned.1.call-done, f32[2,384,384]{2,1,0:T(8,128)S(1)} %fusion.3), kind=kOutput, calls=%fused_computation.3 | convolution fusion | flops 4836753408 | bytes 26345472 | tf_op jit(solution)/shard_map/emf,efd->emd/dot_general | solution.py:55
  177.2 11.1 %copy.35 = bf16[2,384,4096]{2,0,1:T(2,128)(2,1)S(1)} copy(bf16[2,384,4096]{2,1,0:T(8,128)(2,1)} %convolution_convert_fusion) | data formatting | bytes 12582912 | tf_op jit(solution)/shard_map/optimization_barrier | solution.py:56
  188.3 6.1 %copy.36 = bf16[2,4,8,12,4096]{4,0,3,1,2:T(2,128)(2,1)} copy(bf16[2,4,8,12,4096]{4,0,3,2,1:T(2,128)(2,1)S(1)} %bitcast.41) | data formatting | bytes 12582912 | tf_op jit(solution)/shard_map/reshape;broadcast_in_dim | solution.py:58
  194.4 4.9 %all-to-all-start.1 = ((bf16[2,4,8,12,4096]{4,0,3,1,2:T(2,128)(2,1)}), bf16[2,4,8,12,4096]{4,0,3,1,2:T(2,128)(2,1)}, u32[]{:S(2)}, u32[]{:S(2)}) async-start(bf16[2,4,8,12,4096]{4,0,3,1,2:T(2,128)(2,1)} %copy.36), calls=%async_computation.1 | async-start | bytes 12582912 | tf_op jit(solution)/shard_map/all_to_all | solution.py:63
  199.4 13.1 %all-gather = f32[4,16,8]{1,2,0:T(8,128)S(1)} all-gather(f32[1,16,8]{1,2,0:T(8,128)S(1)} %convert_bitcast_fusion.1), channel_id=1, replica_groups=mesh['rep'=4,'exp'=8] {'rep'}, dimensions={0}, use_global_device_ids=true | all-gather | bytes 2560 | tf_op jit(solution)/shard_map/all_gather | solution.py:28
  212.5 0.1 copy.39
  212.6 0.1 eq.72
  212.7 0.1 fusion.14
  212.8 0.3 reduce_window_sum.23
  213.2 0.1 mul.56
  213.3 13.3 %all-gather.1 = f32[4,16,8]{1,2,0:T(8,128)S(1)} all-gather(f32[1,16,8]{1,2,0:T(8,128)S(1)} %bitcast.43), channel_id=1, replica_groups=mesh['rep'=4,'exp'=8] {'rep'}, dimensions={0}, use_global_device_ids=true | all-gather | bytes 2560 | tf_op jit(solution)/shard_map/all_gather | solution.py:27
  226.6 0.2 select_reduce_fusion
  226.9 44.0 %all-to-all-done.1 = bf16[2,4,8,12,4096]{4,0,3,1,2:T(2,128)(2,1)} async-done(((bf16[2,4,8,12,4096]{4,0,3,1,2:T(2,128)(2,1)}), bf16[2,4,8,12,4096]{4,0,3,1,2:T(2,128)(2,1)}, u32[]{:S(2)}, u32[]{:S(2)}) %all-to-all-start.1) | async-done | bytes 6291488 | tf_op jit(solution)/shard_map/all_to_all | solution.py:63
  270.9 11.7 %copy.37 = bf16[8,2,4,1,12,4096]{5,2,4,1,0,3:T(4,128)(2,1)} copy(bf16[8,2,4,1,12,4096]{5,1,4,2,0,3:T(2,128)(2,1)} %bitcast.6) | data formatting | bytes 12582912 | tf_op jit(solution)/shard_map/all_to_all | solution.py:63
  282.6 14.3 %gather_fusion = bf16[512,4096]{1,0:T(8,128)(2,1)} fusion(bf16[16,4,12,4096]{3,1,2,0:T(4,128)(2,1)} %bitcast.40, s32[512]{0:T(512)S(1)} %fusion.21), kind=kCustom, calls=%fused_computation | custom fusion | bytes 8394752 | tf_op jit(solution)/shard_map/gather | solution.py:70
  296.9 6.5 %fusion = f32[4,16,4096]{2,1,0:T(8,128)} fusion(f32[4,16,8]{2,1,0:T(8,128)S(1)} %copy.40, bf16[512,4096]{1,0:T(8,128)(2,1)} %gather_fusion), kind=kLoop, calls=%fused_computation.2 | loop fusion | flops 6029312 | bytes 5244928 | tf_op jit(solution)/shard_map/reduce_sum | solution.py:72
  303.5 23.7 %reduce-scatter.2.cloned.1.call-done = f32[1,16,4096]{2,1,0:T(8,128)} async-done(((f32[4,16,4096]{2,1,0:T(8,128)}), f32[1,16,4096]{2,1,0:T(8,128)}) %reduce-scatter.2.cloned.1.call-update) | async-done | bytes 262160 | tf_op jit(solution)/shard_map/reduce_scatter | solution.py:77
  327.3 1.6 convert_bitcast_fusion
  (19 shorter events, 0.3 us)
Async XLA Ops:
  6.5 1.6 copy-start
  6.5 150.2 %all-gather.4.cloned.1.call-start = ((), (), s32[]{:S(2)}) async-start(), calls=%async_computation.3 | async-start | bytes 7864320 | tf_op jit(solution)/shard_map/all_gather | solution.py:49
  194.4 4.9 %copy-start.2 = (s32[16,8]{0,1:T(8,128)S(1)}, s32[16,8]{0,1:T(8,128)}, u32[]{:S(2)}) copy-start(s32[16,8]{0,1:T(8,128)} %param.7) | copy-start | bytes 1540
  194.4 18.9 %copy-start.3 = (f32[16,8]{0,1:T(8,128)S(1)}, f32[16,8]{0,1:T(8,128)}, u32[]{:S(2)}) copy-start(f32[16,8]{0,1:T(8,128)} %param.8) | copy-start | bytes 1540
  194.4 76.5 %all-to-all-start.1 = ((bf16[2,4,8,12,4096]{4,0,3,1,2:T(2,128)(2,1)}), bf16[2,4,8,12,4096]{4,0,3,1,2:T(2,128)(2,1)}, u32[]{:S(2)}, u32[]{:S(2)}) async-start(bf16[2,4,8,12,4096]{4,0,3,1,2:T(2,128)(2,1)} %copy.36), calls=%async_computation.1 | async-start | bytes 12582912 | tf_op jit(solution)/shard_map/all_to_all | solution.py:63
  199.3 128.0 %reduce-scatter.2.cloned.1.call-start = ((), (), s32[]{:S(2)}) async-start(), calls=%async_computation.4 | async-start | bytes 1310720 | tf_op jit(solution)/shard_map/reduce_scatter | solution.py:77
  282.6 46.3 %copy-start.1 = (bf16[16,4096]{1,0:T(8,128)(2,1)S(1)}, bf16[16,4096]{1,0:T(8,128)(2,1)}, u32[]{:S(2)}) copy-start(bf16[16,4096]{1,0:T(8,128)(2,1)} %param.6) | copy-start | bytes 393220
Sparse Core Ops, SparseCore 0:
  42.0 114.7 all-gather.3
  303.6 23.5 reduce-scatter.1
where the time goes:
time: 336 us
  waiting for transfers between devices  183 us (54%)
  blocking collectives  52.4 us (16%)
  local copies, waits for them, and re-layouts  50.6 us (15%)
  matrix products  22.3 us (7%)
  between operations  13.5 us (4%)
  other arithmetic  9.43 us (3%)
  starting transfers between devices  4.91 us (1%)
    all_gather x1, waiting for transfers between devices, on_device(): rows_now = lax.all_gather(arrived, 'rep', axis=2, tiled=True)[0]  115 us
    all_to_all x1, waiting for transfers between devices, on_device(): lax.all_to_all(outcomes, 'exp', split_axis=2, concat_axis=0, tiled=True)  44 us
    all_to_all x1, blocking collectives, on_device(): lax.all_to_all(buffer, 'exp', split_axis=0, concat_axis=2, tiled=True)  25.9 us
    reduce_scatter x1, waiting for transfers between devices, on_device(): summed = lax.psum_scatter(weighted, 'rep', scatter_dimension=0, tiled=True)  23.7 us
    gather x1, local copies, waits for them, and re-layouts, on_device(): returned[expert_index, replica_index, place_index].astype(jnp.float32)  14.3 us
    all_gather x1, blocking collectives, routing_column(): lax.all_gather(route_weights, 'rep', axis=0, tiled=True)  13.3 us
    all_gather x1, blocking collectives, routing_column(): lax.all_gather(as_float, 'rep', axis=0, tiled=True)  13.1 us
    dot_general x1, matrix products, on_device(): jnp.einsum('emf,efd->emd', hidden, down_weight, preferred_element_type=jn...  12.4 us
  transfers between devices with their start and end apart: 3, of which 3 were waited for; matrix products, arithmetic and copies ran while one was open for 0% of the time, Pallas kernels for 0%

commit v1 on v0

--- a/solution.py
+++ b/solution.py
@@ -30,7 +30,7 @@
     return (weights_all, experts_all.astype(jnp.int32))
 
 
-def on_device(tokens, routed_experts, route_weights, gate_weight, up_weight, down_weight):
+def on_device_slots(tokens, routed_experts, route_weights, gate_weight, up_weight, down_weight):
     replicas = lax.axis_size("rep")
     owners = lax.axis_size("exp")
     token_rows, model_width = tokens.shape
@@ -78,6 +78,80 @@
     return summed.reshape(token_rows, model_width).astype(jnp.bfloat16)
 
 
+def swap_exp(value, bit):
+    owners = lax.axis_size("exp")
+    return lax.ppermute(value, "exp", [(i, i ^ bit) for i in range(owners)])
+
+
+def turn_rep(value, shift):
+    replicas = lax.axis_size("rep")
+    return lax.ppermute(value, "rep", [(i, (i - shift) % replicas) for i in range(replicas)])
+
+
+def add(left, right):
+    return (left.astype(jnp.float32) + right.astype(jnp.float32)).astype(jnp.bfloat16)
+
+
+def on_device_dense(tokens, routed_experts, route_weights, gate_weight, up_weight, down_weight):
+    replicas = lax.axis_size("rep")
+    token_rows, model_width = tokens.shape
+    local_experts, shard_units, _ = gate_weight.shape
+    half = replicas // 2
+    high = route_weights.astype(jnp.bfloat16)
+    low = (route_weights - high.astype(jnp.float32)).astype(jnp.bfloat16)
+    extra = jnp.concatenate([routed_experts.astype(jnp.bfloat16), high, low], axis=1)
+    extra = jnp.pad(extra, ((0, 0), (0, 128 - extra.shape[1])))
+    packed = jnp.concatenate([tokens, extra], axis=1)
+
+    blocks = [packed] + [turn_rep(packed, s) for s in range(1, replicas)]
+    first = jnp.concatenate(blocks[:half], axis=0)
+    second = jnp.concatenate(blocks[half:], axis=0)
+    first = jnp.concatenate([first, swap_exp(first, 2)], axis=0)
+    second = jnp.concatenate([second, swap_exp(second, 4)], axis=0)
+    plane = jnp.concatenate([first, swap_exp(first, 4), second, swap_exp(second, 2)], axis=0)
+    rows = jnp.concatenate([plane, swap_exp(plane, 1)], axis=0)
+
+    own_first = lax.axis_index("exp") * local_experts
+    top = routed_experts.shape[1]
+    names = rows[:, model_width : model_width + top].astype(jnp.int32)
+    scale = rows[:, model_width + top : model_width + 2 * top].astype(jnp.float32) + rows[
+        :, model_width + 2 * top : model_width + 3 * top
+    ].astype(jnp.float32)
+    local = own_first + jnp.arange(local_experts, dtype=jnp.int32)
+    weight = jnp.sum(
+        jnp.where(names[:, None, :] == local[None, :, None], scale[:, None, :], 0.0), axis=2
+    )
+    activations = rows[:, :model_width]
+    gates = gate_weight.reshape(local_experts * shard_units, model_width)
+    ups = up_weight.reshape(local_experts * shard_units, model_width)
+    downs = down_weight.reshape(local_experts * shard_units, model_width)
+    gate_value = jnp.einsum("md,fd->mf", activations, gates, preferred_element_type=jnp.float32)
+    up_value = jnp.einsum("md,fd->mf", activations, ups, preferred_element_type=jnp.float32)
+    unit_weight = jnp.repeat(weight, shard_units, axis=1)
+    hidden = (jax.nn.silu(gate_value) * up_value * unit_weight).astype(jnp.bfloat16)
+    partial = jnp.dot(hidden, downs, preferred_element_type=jnp.float32).astype(jnp.bfloat16)
+
+    size = partial.shape[0] // 2
+    plane = add(partial[:size], swap_exp(partial[size:], 1))
+    size = size // 2
+    first, second = plane[:size], plane[size:]
+    size = size // 2
+    first, second = (
+        add(first[:size], swap_exp(first[size:], 4)),
+        add(second[:size], swap_exp(second[size:], 2)),
+    )
+    size = size // 2
+    first, second = (
+        add(first[:size], swap_exp(first[size:], 2)),
+        add(second[:size], swap_exp(second[size:], 4)),
+    )
+    column = jnp.concatenate([first, second], axis=0).reshape(replicas, token_rows, model_width)
+    total = column[0].astype(jnp.float32)
+    for s in range(1, replicas):
+        total = total + turn_rep(column[s], -s).astype(jnp.float32)
+    return total.astype(jnp.bfloat16)
+
+
 def solution(mesh):
     placed = (
         P(("rep", "exp"), None),
@@ -87,6 +161,11 @@
         P("exp", "rep", None),
         P("exp", "rep", None),
     )
+    plane = mesh.shape["exp"] == 8
     return jax.shard_map(
-        on_device, mesh=mesh, in_specs=placed, out_specs=P(("rep", "exp"), None), check_vma=False
+        on_device_dense if plane else on_device_slots,
+        mesh=mesh,
+        in_specs=placed,
+        out_specs=P(("rep", "exp"), None),
+        check_vma=False,
     )

time: 336 us -> 141 us (0.42)
  waiting for transfers between devices: 183 us -> 42.8 us
  blocking collectives: 52.4 us -> 0 us
  starting transfers between devices: 4.91 us -> 27.2 us
  between operations: 13.5 us -> 0.16 us
  local copies, waits for them, and re-layouts: 50.6 us -> 39.4 us
    all_gather x1 -> x0, waiting for transfers between devices: 115 us -> none  [on_device(): rows_now = lax.all_gather(arrived, 'rep', axis=2, tiled=True)[0]]
    all_to_all x1 -> x0, waiting for transfers between devices: 44 us -> none  [on_device(): lax.all_to_all(outcomes, 'exp', split_axis=2, concat_axis=0, tiled=True)]
    ppermute x0 -> x16, waiting for transfers between devices: none -> 42.8 us  [the longest x10 32.3 us: swap_exp(): return lax.ppermute(value, 'exp', [(i, i ^ bit) for i in range(owners)])]
    ppermute x0 -> x16, starting transfers between devices: none -> 27.2 us  [the longest x6 17.6 us: turn_rep(): lax.ppermute(value, 'rep', [(i, (i - shift) % replicas) for i in range(re...]
    all_gather x2 -> x0, blocking collectives: 26.4 us -> none  [the longest x1 13.3 us: routing_column(): lax.all_gather(route_weights, 'rep', axis=0, tiled=True)]
    all_to_all x1 -> x0, blocking collectives: 25.9 us -> none  [on_device(): lax.all_to_all(buffer, 'exp', split_axis=0, concat_axis=2, tiled=True)]
    reduce_scatter x1 -> x0, waiting for transfers between devices: 23.7 us -> none  [on_device(): summed = lax.psum_scatter(weighted, 'rep', scatter_dimension=0, tiled=True)]
    concatenate x0 -> x3, local copies, waits for them, and re-layouts: none -> 21.8 us  [the longest x1 12.2 us: on_device_dense(): rows = jnp.concatenate([plane, swap_exp(plane, 1)], axis=0)]
  transfers between devices with their start and end apart: 3 -> 16, of which waited for: 3 -> 10; matrix products, arithmetic and copies ran while one was open for 0% -> 9% of each run, Pallas kernels for 0% -> 0%
where the time goes in v1:
time: 141 us; the launch traced here: 139 us
  waiting for transfers between devices  42.8 us (30%)
  local copies, waits for them, and re-layouts  39.4 us (28%)
  starting transfers between devices  27.2 us (19%)
  matrix products  22.5 us (16%)
  other arithmetic  7.16 us (5%)
    ppermute x10, waiting for transfers between devices, swap_exp(): return lax.ppermute(value, 'exp', [(i, i ^ bit) for i in range(owners)])  32.3 us
    ppermute x6, starting transfers between devices, turn_rep(): lax.ppermute(value, 'rep', [(i, (i - shift) % replicas) for i in range(re...  17.6 us
    dot_general x1, matrix products, on_device_dense(): jnp.dot(hidden, downs, preferred_element_type=jnp.float32)  16.7 us
    concatenate x1, local copies, waits for them, and re-layouts, on_device_dense(): rows = jnp.concatenate([plane, swap_exp(plane, 1)], axis=0)  12.2 us
    ppermute x6, waiting for transfers between devices, turn_rep(): lax.ppermute(value, 'rep', [(i, (i - shift) % replicas) for i in range(re...  10.5 us
    ppermute x10, starting transfers between devices, swap_exp(): return lax.ppermute(value, 'exp', [(i, i ^ bit) for i in range(owners)])  9.59 us
    ppermute x4, local copies, waits for them, and re-layouts, swap_exp(): return lax.ppermute(value, 'exp', [(i, i ^ bit) for i in range(owners)])  9.26 us
    concatenate x1, local copies, waits for them, and re-layouts, on_device_dense(): jnp.concatenate([first, swap_exp(first, 4), second, swap_exp(second, 2)],...  9.05 us
  transfers between devices with their start and end apart: 16, of which 10 were waited for; matrix products, arithmetic and copies ran while one was open for 9% of the time, Pallas kernels for 0%

profile of v1, /device:TPU:0, one launch (start us, length us, event | category | flops | bytes accessed | tf_op | source)
XLA Modules:
  0.0 139.3 jit_solution(17643534562204459503)
XLA Ops:
  2.6 4.1 %collective-permute-start.3 = (bf16[16,4224]{1,0:T(8,128)(2,1)S(1)}, bf16[16,4224]{1,0:T(8,128)(2,1)S(1)}, u32[]{:S(2)}, u32[]{:S(2)}) collective-permute-start(bf16[16,4224]{1,0:T(8,128)(2,1)S(1)} %pad_maximum_fusion.4), channel_id=1, source_target_pairs={{0,16},{8,24},{16,0},{24,8},{1,17},{9,25},{17,1},{25,9},{2,18},{10... | collective-permute-start | bytes 405512 | tf_op jit(solution)/shard_map/ppermute | solution.py:88
  6.7 1.6 %collective-permute-start.4 = (bf16[16,4224]{1,0:T(8,128)(2,1)S(1)}, bf16[16,4224]{1,0:T(8,128)(2,1)S(1)}, u32[]{:S(2)}, u32[]{:S(2)}) collective-permute-start(bf16[16,4224]{1,0:T(8,128)(2,1)S(1)} %pad_maximum_fusion.4), channel_id=1, source_target_pairs={{0,8},{8,16},{16,24},{24,0},{1,9},{9,17},{17,25},{25,1},{2,10},{10... | collective-permute-start | bytes 405512 | tf_op jit(solution)/shard_map/ppermute | solution.py:88
  8.2 2.2 %collective-permute-start = (bf16[16,4224]{1,0:T(8,128)(2,1)S(1)}, bf16[16,4224]{1,0:T(8,128)(2,1)S(1)}, u32[]{:S(2)}, u32[]{:S(2)}) collective-permute-start(bf16[16,4224]{1,0:T(8,128)(2,1)S(1)} %pad_maximum_fusion.4), channel_id=1, source_target_pairs={{0,24},{8,0},{16,8},{24,16},{1,25},{9,1},{17,9},{25,17},{2,26},{10... | collective-permute-start | bytes 405512 | tf_op jit(solution)/shard_map/ppermute | solution.py:88
  10.5 6.4 %collective-permute-done.3 = bf16[16,4224]{1,0:T(8,128)(2,1)S(1)} collective-permute-done((bf16[16,4224]{1,0:T(8,128)(2,1)S(1)}, bf16[16,4224]{1,0:T(8,128)(2,1)S(1)}, u32[]{:S(2)}, u32[]{:S(2)}) %collective-permute-start.3) | collective-permute-done | bytes 135200 | tf_op jit(solution)/shard_map/ppermute | solution.py:88
  17.0 1.9 %collective-permute-start.5 = (bf16[32,4224]{1,0:T(8,128)(2,1)S(1)}, bf16[32,4224]{1,0:T(8,128)(2,1)S(1)}, u32[]{:S(2)}, u32[]{:S(2)}) collective-permute-start(bf16[32,4224]{1,0:T(8,128)(2,1)S(1)} %pad_maximum_fusion.3), channel_id=1, source_target_pairs={{0,4},{1,5},{2,6},{3,7},{4,0},{5,1},{6,2},{7,3},{8,12},{9,13},{10,... | collective-permute-start | bytes 811016 | tf_op jit(solution)/shard_map/ppermute | solution.py:83
  19.8 1.6 %collective-permute-start.1 = (bf16[32,4224]{1,0:T(8,128)(2,1)S(1)}, bf16[32,4224]{1,0:T(8,128)(2,1)S(1)}, u32[]{:S(2)}, u32[]{:S(2)}) collective-permute-start(bf16[32,4224]{1,0:T(8,128)(2,1)S(1)} %pad_maximum_fusion.2), channel_id=1, source_target_pairs={{0,2},{1,3},{2,0},{3,1},{4,6},{5,7},{6,4},{7,5},{8,10},{9,11},{10,... | collective-permute-start | bytes 811016 | tf_op jit(solution)/shard_map/ppermute | solution.py:83
  21.4 2.5 %collective-permute-done.5 = bf16[32,4224]{1,0:T(8,128)(2,1)S(1)} collective-permute-done((bf16[32,4224]{1,0:T(8,128)(2,1)S(1)}, bf16[32,4224]{1,0:T(8,128)(2,1)S(1)}, u32[]{:S(2)}, u32[]{:S(2)}) %collective-permute-start.5) | collective-permute-done | bytes 270368 | tf_op jit(solution)/shard_map/ppermute | solution.py:83
  24.8 1.5 %collective-permute-start.6 = (bf16[64,4224]{1,0:T(8,128)(2,1)}, bf16[64,4224]{1,0:T(8,128)(2,1)}, u32[]{:S(2)}, u32[]{:S(2)}) collective-permute-start(bf16[64,4224]{1,0:T(8,128)(2,1)} %pad_maximum_fusion.1), channel_id=1, source_target_pairs={{0,2},{1,3},{2,0},{3,1},{4,6},{5,7},{6,4},{7,5},{8,10},{9,11},{10,... | collective-permute-start | bytes 1622024 | tf_op jit(solution)/shard_map/ppermute | solution.py:83
  26.2 1.3 collective-permute-done.1
  30.2 1.4 copy.30
  31.6 2.4 %copy.31 = bf16[32,4224]{0,1:T(8,128)(2,1)} copy(bf16[32,4224]{1,0:T(8,128)(2,1)} %copy-done.3) | data formatting | bytes 540672 | tf_op jit(solution)/shard_map/ppermute | solution.py:83
  34.0 2.3 %copy.27 = bf16[32,4224]{0,1:T(8,128)(2,1)} copy(bf16[32,4224]{1,0:T(8,128)(2,1)} %copy-done.4) | data formatting | bytes 540672 | tf_op jit(solution)/shard_map/ppermute | solution.py:83
  36.4 1.7 %collective-permute-done.6 = bf16[64,4224]{1,0:T(8,128)(2,1)} collective-permute-done((bf16[64,4224]{1,0:T(8,128)(2,1)}, bf16[64,4224]{1,0:T(8,128)(2,1)}, u32[]{:S(2)}, u32[]{:S(2)}) %collective-permute-start.6) | collective-permute-done | bytes 540704 | tf_op jit(solution)/shard_map/ppermute | solution.py:83
  38.0 2.3 %copy.32 = bf16[64,4224]{0,1:T(8,128)(2,1)} copy(bf16[64,4224]{1,0:T(8,128)(2,1)} %collective-permute-done.6) | data formatting | bytes 1081344 | tf_op jit(solution)/shard_map/ppermute | solution.py:83
  40.3 2.2 %copy.28 = bf16[64,4224]{0,1:T(8,128)(2,1)} copy(bf16[64,4224]{1,0:T(8,128)(2,1)} %collective-permute-done.2) | data formatting | bytes 1081344 | tf_op jit(solution)/shard_map/ppermute | solution.py:83
  42.5 9.0 %concatenate.35 = bf16[256,4224]{0,1:T(8,128)(2,1)} concatenate(bf16[16,4224]{0,1:T(8,128)(2,1)S(1)} %copy.25, bf16[16,4224]{0,1:T(8,128)(2,1)S(1)} %copy.26, bf16[32,4224]{0,1:T(8,128)(2,1)} %copy.27, bf16[64,4224]{0,1:T(8,128)(2,1)} %copy.28, bf16[16,4224]{0,1:T(8,128)(2,1)S(1)} %copy.29, bf16[16,4224]{0,1:T(8,128)(2,1)} %copy.30, bf16[32,4224]{0,1:T(8,128)(2,1)} %copy.31, ...), dimensions={0} | concatenate | bytes 4325376 | tf_op jit(solution)/shard_map/concatenate | solution.py:111
  51.6 4.6 %collective-permute-done.7 = bf16[256,4224]{0,1:T(8,128)(2,1)} collective-permute-done((bf16[256,4224]{0,1:T(8,128)(2,1)}, bf16[256,4224]{0,1:T(8,128)(2,1)}, u32[]{:S(2)}, u32[]{:S(2)}) %collective-permute-start.7) | collective-permute-done | bytes 2162720 | tf_op jit(solution)/shard_map/ppermute | solution.py:83
  56.2 12.2 %concatenate.36 = bf16[512,4224]{0,1:T(8,128)(2,1)} concatenate(bf16[16,4224]{0,1:T(8,128)(2,1)S(1)} %copy.25, bf16[16,4224]{0,1:T(8,128)(2,1)S(1)} %copy.26, bf16[32,4224]{0,1:T(8,128)(2,1)} %copy.27, bf16[64,4224]{0,1:T(8,128)(2,1)} %copy.28, bf16[16,4224]{0,1:T(8,128)(2,1)S(1)} %copy.29, bf16[16,4224]{0,1:T(8,128)(2,1)} %copy.30, bf16[32,4224]{0,1:T(8,128)(2,1)} %copy.31, ...), dimensions={0} | concatenate | bytes 8650752 | tf_op jit(solution)/shard_map/concatenate | solution.py:112
  70.8 1.5 %copy-done = bf16[512,4224]{0,1:T(8,128)(2,1)S(1)} copy-done((bf16[512,4224]{0,1:T(8,128)(2,1)S(1)}, bf16[512,4224]{0,1:T(8,128)(2,1)}, u32[]{:S(2)}) %copy-start) | copy-done | bytes 4325400
  72.3 5.8 %fusion = f32[512,768]{1,0:T(8,128)S(1)} fusion(bf16[768,4096]{1,0:T(8,128)(2,1)} %bitcast.14, bf16[512,4224]{0,1:T(8,128)(2,1)S(1)} %copy-done), kind=kOutput, calls=%fused_computation.2 | convolution fusion | flops 3221225472 | bytes 12058624 | tf_op jit(solution)/shard_map/md,fd->mf/dot_general | solution.py:129
  78.1 16.7 %convolution_convert_fusion = bf16[512,4096]{1,0:T(8,128)(2,1)} fusion(bf16[768,4096]{1,0:T(8,128)(2,1)} %bitcast.15, f32[512,768]{1,0:T(8,128)S(1)} %bitcast.13, f32[512,768]{1,0:T(8,128)S(1)} %fusion, bf16[768,4096]{1,0:T(8,128)(2,1)} %bitcast.16, bf16[512,4224]{0,1:T(8,128)(2,1)} %concatenate.36), kind=kOutput, calls=%fused_computation | convolution fusion | flops 6447300608 | bytes 24117248 | tf_op jit(solution)/shard_map/dot_general | solution.py:132
  94.8 1.9 %slice.91 = bf16[256,4096]{1,0:T(8,128)(2,1)S(1)} slice(bf16[512,4096]{1,0:T(8,128)(2,1)} %convolution_convert_fusion), slice={[256:512], [0:4096]} | slice | bytes 4194304 | tf_op jit(solution)/shard_map/slice | solution.py:135
  96.9 4.0 %collective-permute-done.8 = bf16[256,4096]{1,0:T(8,128)(2,1)S(1)} collective-permute-done((bf16[256,4096]{1,0:T(8,128)(2,1)S(1)}, bf16[256,4096]{1,0:T(8,128)(2,1)S(1)}, u32[]{:S(2)}, u32[]{:S(2)}) %collective-permute-start.8) | collective-permute-done | bytes 2097184 | tf_op jit(solution)/shard_map/ppermute | solution.py:83
  101.8 1.6 %collective-permute-start.12 = (bf16[64,4096]{1,0:T(8,128)(2,1)S(1)}, bf16[64,4096]{1,0:T(8,128)(2,1)S(1)}, u32[]{:S(2)}, u32[]{:S(2)}) collective-permute-start(bf16[64,4096]{1,0:T(8,128)(2,1)S(1)} %get-tuple-element.10), channel_id=1, source_target_pairs={{0,2},{1,3},{2,0},{3,1},{4,6},{5,7},{6,4},{7,5},{8,10},{9,11},{10,... | collective-permute-start | bytes 1572872 | tf_op jit(solution)/shard_map/ppermute | solution.py:83
  103.4 1.1 collective-permute-start.9
  104.5 11.4 %collective-permute-done.12 = bf16[64,4096]{1,0:T(8,128)(2,1)S(1)} collective-permute-done((bf16[64,4096]{1,0:T(8,128)(2,1)S(1)}, bf16[64,4096]{1,0:T(8,128)(2,1)S(1)}, u32[]{:S(2)}, u32[]{:S(2)}) %collective-permute-start.12) | collective-permute-done | bytes 524320 | tf_op jit(solution)/shard_map/ppermute | solution.py:83
  115.9 1.2 collective-permute-done.9
  119.0 5.7 %collective-permute-done.10 = bf16[32,4096]{1,0:T(8,128)(2,1)S(1)} collective-permute-done((bf16[32,4096]{1,0:T(8,128)(2,1)S(1)}, bf16[32,4096]{1,0:T(8,128)(2,1)S(1)}, u32[]{:S(2)}, u32[]{:S(2)}) %collective-permute-start.10) | collective-permute-done | bytes 262176 | tf_op jit(solution)/shard_map/ppermute | solution.py:83
  124.7 4.8 %collective-permute-start.11 = (bf16[16,4096]{1,0:T(8,128)(2,1)S(1)}, bf16[16,4096]{1,0:T(8,128)(2,1)S(1)}, u32[]{:S(2)}, u32[]{:S(2)}) collective-permute-start(bf16[16,4096]{1,0:T(8,128)(2,1)S(1)} %slice.97), channel_id=1, source_target_pairs={{0,8},{8,16},{16,24},{24,0},{1,9},{9,17},{17,25},{25,1},{2,10},{10... | collective-permute-start | bytes 393224 | tf_op jit(solution)/shard_map/ppermute | solution.py:88
  129.6 2.2 %collective-permute-start.14 = (bf16[16,4096]{1,0:T(8,128)(2,1)S(1)}, bf16[16,4096]{1,0:T(8,128)(2,1)S(1)}, u32[]{:S(2)}, u32[]{:S(2)}) collective-permute-start(bf16[16,4096]{1,0:T(8,128)(2,1)S(1)} %get-tuple-element.11), channel_id=1, source_target_pairs={{0,16},{8,24},{16,0},{24,8},{1,17},{9,25},{17,1},{25,9},{2,18},{10... | collective-permute-start | bytes 393224 | tf_op jit(solution)/shard_map/ppermute | solution.py:88
  131.8 2.7 %collective-permute-start.15 = (bf16[16,4096]{1,0:T(8,128)(2,1)S(1)}, bf16[16,4096]{1,0:T(8,128)(2,1)S(1)}, u32[]{:S(2)}, u32[]{:S(2)}) collective-permute-start(bf16[16,4096]{1,0:T(8,128)(2,1)S(1)} %get-tuple-element.12), channel_id=1, source_target_pairs={{0,24},{8,0},{16,8},{24,16},{1,25},{9,1},{17,9},{25,17},{2,26},{10... | collective-permute-start | bytes 393224 | tf_op jit(solution)/shard_map/ppermute | solution.py:88
  134.5 4.1 %collective-permute-done.14 = bf16[16,4096]{1,0:T(8,128)(2,1)S(1)} collective-permute-done((bf16[16,4096]{1,0:T(8,128)(2,1)S(1)}, bf16[16,4096]{1,0:T(8,128)(2,1)S(1)}, u32[]{:S(2)}, u32[]{:S(2)}) %collective-permute-start.14) | collective-permute-done | bytes 131104 | tf_op jit(solution)/shard_map/ppermute | solution.py:88
  (50 shorter events, 13.3 us)
Async XLA Ops:
  0.0 27.5 %copy-start.2 = (bf16[16,4096]{1,0:T(8,128)(2,1)S(1)}, bf16[16,4096]{1,0:T(8,128)(2,1)}, u32[]{:S(2)}) copy-start(bf16[16,4096]{1,0:T(8,128)(2,1)} %param.6) | copy-start | bytes 393220
  2.6 14.4 %collective-permute-start.3 = (bf16[16,4224]{1,0:T(8,128)(2,1)S(1)}, bf16[16,4224]{1,0:T(8,128)(2,1)S(1)}, u32[]{:S(2)}, u32[]{:S(2)}) collective-permute-start(bf16[16,4224]{1,0:T(8,128)(2,1)S(1)} %pad_maximum_fusion.4), channel_id=1, source_target_pairs={{0,16},{8,24},{16,0},{24,8},{1,17},{9,25},{17,1},{25,9},{2,18},{10... | collective-permute-start | bytes 405512 | tf_op jit(solution)/shard_map/ppermute | solution.py:88
  6.7 10.3 %collective-permute-start.4 = (bf16[16,4224]{1,0:T(8,128)(2,1)S(1)}, bf16[16,4224]{1,0:T(8,128)(2,1)S(1)}, u32[]{:S(2)}, u32[]{:S(2)}) collective-permute-start(bf16[16,4224]{1,0:T(8,128)(2,1)S(1)} %pad_maximum_fusion.4), channel_id=1, source_target_pairs={{0,8},{8,16},{16,24},{24,0},{1,9},{9,17},{17,25},{25,1},{2,10},{10... | collective-permute-start | bytes 405512 | tf_op jit(solution)/shard_map/ppermute | solution.py:88
  8.2 10.6 %collective-permute-start = (bf16[16,4224]{1,0:T(8,128)(2,1)S(1)}, bf16[16,4224]{1,0:T(8,128)(2,1)S(1)}, u32[]{:S(2)}, u32[]{:S(2)}) collective-permute-start(bf16[16,4224]{1,0:T(8,128)(2,1)S(1)} %pad_maximum_fusion.4), channel_id=1, source_target_pairs={{0,24},{8,0},{16,8},{24,16},{1,25},{9,1},{17,9},{25,17},{2,26},{10... | collective-permute-start | bytes 405512 | tf_op jit(solution)/shard_map/ppermute | solution.py:88
  17.0 6.9 %collective-permute-start.5 = (bf16[32,4224]{1,0:T(8,128)(2,1)S(1)}, bf16[32,4224]{1,0:T(8,128)(2,1)S(1)}, u32[]{:S(2)}, u32[]{:S(2)}) collective-permute-start(bf16[32,4224]{1,0:T(8,128)(2,1)S(1)} %pad_maximum_fusion.3), channel_id=1, source_target_pairs={{0,4},{1,5},{2,6},{3,7},{4,0},{5,1},{6,2},{7,3},{8,12},{9,13},{10,... | collective-permute-start | bytes 811016 | tf_op jit(solution)/shard_map/ppermute | solution.py:83
  19.8 7.7 %collective-permute-start.1 = (bf16[32,4224]{1,0:T(8,128)(2,1)S(1)}, bf16[32,4224]{1,0:T(8,128)(2,1)S(1)}, u32[]{:S(2)}, u32[]{:S(2)}) collective-permute-start(bf16[32,4224]{1,0:T(8,128)(2,1)S(1)} %pad_maximum_fusion.2), channel_id=1, source_target_pairs={{0,2},{1,3},{2,0},{3,1},{4,6},{5,7},{6,4},{7,5},{8,10},{9,11},{10,... | collective-permute-start | bytes 811016 | tf_op jit(solution)/shard_map/ppermute | solution.py:83
  23.9 5.3 %copy-start.3 = (bf16[32,4224]{1,0:T(8,128)(2,1)}, bf16[32,4224]{1,0:T(8,128)(2,1)S(1)}, u32[]{:S(2)}) copy-start(bf16[32,4224]{1,0:T(8,128)(2,1)S(1)} %collective-permute-done.5) | copy-start | bytes 811012
  24.8 13.3 %collective-permute-start.6 = (bf16[64,4224]{1,0:T(8,128)(2,1)}, bf16[64,4224]{1,0:T(8,128)(2,1)}, u32[]{:S(2)}, u32[]{:S(2)}) collective-permute-start(bf16[64,4224]{1,0:T(8,128)(2,1)} %pad_maximum_fusion.1), channel_id=1, source_target_pairs={{0,2},{1,3},{2,0},{3,1},{4,6},{5,7},{6,4},{7,5},{8,10},{9,11},{10,... | collective-permute-start | bytes 1622024 | tf_op jit(solution)/shard_map/ppermute | solution.py:83
  27.5 1.7 %copy-start.4 = (bf16[32,4224]{1,0:T(8,128)(2,1)}, bf16[32,4224]{1,0:T(8,128)(2,1)S(1)}, u32[]{:S(2)}) copy-start(bf16[32,4224]{1,0:T(8,128)(2,1)S(1)} %collective-permute-done.1) | copy-start | bytes 811012
  28.4 11.9 %collective-permute-start.2 = (bf16[64,4224]{1,0:T(8,128)(2,1)}, bf16[64,4224]{1,0:T(8,128)(2,1)}, u32[]{:S(2)}, u32[]{:S(2)}) collective-permute-start(bf16[64,4224]{1,0:T(8,128)(2,1)} %pad_maximum_fusion), channel_id=1, source_target_pairs={{0,4},{1,5},{2,6},{3,7},{4,0},{5,1},{6,2},{7,3},{8,12},{9,13},{10,... | collective-permute-start | bytes 1622024 | tf_op jit(solution)/shard_map/ppermute | solution.py:83
  51.6 4.6 %collective-permute-start.7 = (bf16[256,4224]{0,1:T(8,128)(2,1)}, bf16[256,4224]{0,1:T(8,128)(2,1)}, u32[]{:S(2)}, u32[]{:S(2)}) collective-permute-start(bf16[256,4224]{0,1:T(8,128)(2,1)} %concatenate.35), channel_id=1, source_target_pairs={{0,1},{1,0},{2,3},{3,2},{4,5},{5,4},{6,7},{7,6},{8,9},{9,8},{10,11... | collective-permute-start | bytes 6488072 | tf_op jit(solution)/shard_map/ppermute | solution.py:83
  70.1 2.2 %copy-start = (bf16[512,4224]{0,1:T(8,128)(2,1)S(1)}, bf16[512,4224]{0,1:T(8,128)(2,1)}, u32[]{:S(2)}) copy-start(bf16[512,4224]{0,1:T(8,128)(2,1)} %concatenate.36) | copy-start | bytes 12976132
  94.8 6.1 %copy-start.1 = (bf16[512,4096]{1,0:T(8,128)(2,1)S(1)}, bf16[512,4096]{1,0:T(8,128)(2,1)}, u32[]{:S(2)}) copy-start(bf16[512,4096]{1,0:T(8,128)(2,1)} %convolution_convert_fusion) | copy-start | bytes 12582916
  96.7 4.2 %collective-permute-start.8 = (bf16[256,4096]{1,0:T(8,128)(2,1)S(1)}, bf16[256,4096]{1,0:T(8,128)(2,1)S(1)}, u32[]{:S(2)}, u32[]{:S(2)}) collective-permute-start(bf16[256,4096]{1,0:T(8,128)(2,1)S(1)} %slice.91), channel_id=1, source_target_pairs={{0,1},{1,0},{2,3},{3,2},{4,5},{5,4},{6,7},{7,6},{8,9},{9,8},{10,11... | collective-permute-start | bytes 6291464 | tf_op jit(solution)/shard_map/ppermute | solution.py:83
  101.8 14.0 %collective-permute-start.12 = (bf16[64,4096]{1,0:T(8,128)(2,1)S(1)}, bf16[64,4096]{1,0:T(8,128)(2,1)S(1)}, u32[]{:S(2)}, u32[]{:S(2)}) collective-permute-start(bf16[64,4096]{1,0:T(8,128)(2,1)S(1)} %get-tuple-element.10), channel_id=1, source_target_pairs={{0,2},{1,3},{2,0},{3,1},{4,6},{5,7},{6,4},{7,5},{8,10},{9,11},{10,... | collective-permute-start | bytes 1572872 | tf_op jit(solution)/shard_map/ppermute | solution.py:83
  103.4 13.7 %collective-permute-start.9 = (bf16[64,4096]{1,0:T(8,128)(2,1)S(1)}, bf16[64,4096]{1,0:T(8,128)(2,1)S(1)}, u32[]{:S(2)}, u32[]{:S(2)}) collective-permute-start(bf16[64,4096]{1,0:T(8,128)(2,1)S(1)} %get-tuple-element.9), channel_id=1, source_target_pairs={{0,4},{1,5},{2,6},{3,7},{4,0},{5,1},{6,2},{7,3},{8,12},{9,13},{10,... | collective-permute-start | bytes 1572872 | tf_op jit(solution)/shard_map/ppermute | solution.py:83
  117.4 7.3 %collective-permute-start.10 = (bf16[32,4096]{1,0:T(8,128)(2,1)S(1)}, bf16[32,4096]{1,0:T(8,128)(2,1)S(1)}, u32[]{:S(2)}, u32[]{:S(2)}) collective-permute-start(bf16[32,4096]{1,0:T(8,128)(2,1)S(1)} %slice.95), channel_id=1, source_target_pairs={{0,2},{1,3},{2,0},{3,1},{4,6},{5,7},{6,4},{7,5},{8,10},{9,11},{10,... | collective-permute-start | bytes 786440 | tf_op jit(solution)/shard_map/ppermute | solution.py:83
  118.0 11.5 %collective-permute-start.13 = (bf16[32,4096]{1,0:T(8,128)(2,1)S(1)}, bf16[32,4096]{1,0:T(8,128)(2,1)S(1)}, u32[]{:S(2)}, u32[]{:S(2)}) collective-permute-start(bf16[32,4096]{1,0:T(8,128)(2,1)S(1)} %slice.101), channel_id=1, source_target_pairs={{0,4},{1,5},{2,6},{3,7},{4,0},{5,1},{6,2},{7,3},{8,12},{9,13},{10,... | collective-permute-start | bytes 786440 | tf_op jit(solution)/shard_map/ppermute | solution.py:83
  124.7 9.8 %collective-permute-start.11 = (bf16[16,4096]{1,0:T(8,128)(2,1)S(1)}, bf16[16,4096]{1,0:T(8,128)(2,1)S(1)}, u32[]{:S(2)}, u32[]{:S(2)}) collective-permute-start(bf16[16,4096]{1,0:T(8,128)(2,1)S(1)} %slice.97), channel_id=1, source_target_pairs={{0,8},{8,16},{16,24},{24,0},{1,9},{9,17},{17,25},{25,1},{2,10},{10... | collective-permute-start | bytes 393224 | tf_op jit(solution)/shard_map/ppermute | solution.py:88
  129.6 9.0 %collective-permute-start.14 = (bf16[16,4096]{1,0:T(8,128)(2,1)S(1)}, bf16[16,4096]{1,0:T(8,128)(2,1)S(1)}, u32[]{:S(2)}, u32[]{:S(2)}) collective-permute-start(bf16[16,4096]{1,0:T(8,128)(2,1)S(1)} %get-tuple-element.11), channel_id=1, source_target_pairs={{0,16},{8,24},{16,0},{24,8},{1,17},{9,25},{17,1},{25,9},{2,18},{10... | collective-permute-start | bytes 393224 | tf_op jit(solution)/shard_map/ppermute | solution.py:88
  131.8 6.7 %collective-permute-start.15 = (bf16[16,4096]{1,0:T(8,128)(2,1)S(1)}, bf16[16,4096]{1,0:T(8,128)(2,1)S(1)}, u32[]{:S(2)}, u32[]{:S(2)}) collective-permute-start(bf16[16,4096]{1,0:T(8,128)(2,1)S(1)} %get-tuple-element.12), channel_id=1, source_target_pairs={{0,24},{8,0},{16,8},{24,16},{1,25},{9,1},{17,9},{25,17},{2,26},{10... | collective-permute-start | bytes 393224 | tf_op jit(solution)/shard_map/ppermute | solution.py:88

commit v2 on v0

--- a/solution.py
+++ b/solution.py
@@ -1,6 +1,10 @@
+import functools
+
 import jax
 import jax.numpy as jnp
 from jax import lax
+from jax.experimental import pallas as pl
+from jax.experimental.pallas import tpu as pltpu
 from jax.sharding import PartitionSpec as P
 
 
@@ -30,7 +34,7 @@
     return (weights_all, experts_all.astype(jnp.int32))
 
 
-def on_device(tokens, routed_experts, route_weights, gate_weight, up_weight, down_weight):
+def on_device_slots(tokens, routed_experts, route_weights, gate_weight, up_weight, down_weight):
     replicas = lax.axis_size("rep")
     owners = lax.axis_size("exp")
     token_rows, model_width = tokens.shape
@@ -78,6 +82,162 @@
     return summed.reshape(token_rows, model_width).astype(jnp.bfloat16)
 
 
+def expert_kernel(pieces_in, pieces_out, local_experts, shard_units, model_width, top, block, *refs):
+    own_ref, refs = refs[0], refs[1:]
+    ins, refs = refs[: len(pieces_in)], refs[len(pieces_in) :]
+    (gate_hbm, up_hbm, down_hbm), refs = refs[:3], refs[3:]
+    outs, refs = refs[: len(pieces_out)], refs[len(pieces_out) :]
+    rows, gates, ups, downs, hidden, result, row_sem, gate_sem, up_sem, down_sem, out_sem = refs
+    units = local_experts * shard_units
+    unit_block = gates.shape[1]
+    unit_blocks = units // unit_block
+    column_blocks = model_width // block
+
+    row_copies, start = [], 0
+    for place, count in enumerate(pieces_in):
+        row_copies.append(
+            pltpu.make_async_copy(ins[place], rows.at[pl.ds(start, count)], row_sem.at[place])
+        )
+        start += count
+
+    def weight_copies(step):
+        span = pl.ds(step * unit_block, unit_block)
+        return (
+            pltpu.make_async_copy(gate_hbm.at[span], gates.at[step], gate_sem.at[step]),
+            pltpu.make_async_copy(up_hbm.at[span], ups.at[step], up_sem.at[step]),
+        )
+
+    for copy in row_copies:
+        copy.start()
+    for step in range(unit_blocks):
+        for copy in weight_copies(step):
+            copy.start()
+    down_copy = pltpu.make_async_copy(down_hbm, downs, down_sem)
+    down_copy.start()
+    for copy in row_copies:
+        copy.wait()
+
+    extra = rows[:, model_width:].astype(jnp.float32)
+    width = extra.shape[1]
+    scale = pltpu.roll(extra, width - top, 1) + pltpu.roll(extra, width - 2 * top, 1)
+    lane = lax.broadcasted_iota(jnp.int32, extra.shape, 1)
+    weights = []
+    for expert in range(local_experts):
+        name = (own_ref[0] + expert).astype(jnp.float32)
+        chosen = jnp.logical_and(lane < top, extra == name)
+        weights.append(jnp.sum(jnp.where(chosen, scale, 0.0), axis=1, keepdims=True))
+
+    def unit_step(step, carry):
+        for copy in weight_copies(step):
+            copy.wait()
+        values = rows[:, :model_width]
+        contract = (((1,), (1,)), ((), ()))
+        gate = lax.dot_general(values, gates[step], contract, preferred_element_type=jnp.float32)
+        up = lax.dot_general(values, ups[step], contract, preferred_element_type=jnp.float32)
+        unit = step * unit_block + lax.broadcasted_iota(jnp.int32, gate.shape, 1)
+        weight = weights[0]
+        for expert in range(1, local_experts):
+            weight = jnp.where(unit >= expert * shard_units, weights[expert], weight)
+        active = gate / (1.0 + jnp.exp(-gate)) * up * weight
+        hidden[step] = active.astype(jnp.bfloat16)
+        return carry
+
+    lax.fori_loop(0, unit_blocks, unit_step, 0)
+    down_copy.wait()
+    active = jnp.concatenate([hidden[step] for step in range(unit_blocks)], axis=1)
+
+    def out_copies(step):
+        span = pl.ds(pl.multiple_of(step * block, block), block)
+        copies, begin = [], 0
+        for place, count in enumerate(pieces_out):
+            copies.append(
+                pltpu.make_async_copy(
+                    result.at[pl.ds(begin, count), span], outs[place].at[:, span], out_sem.at[step, place]
+                )
+            )
+            begin += count
+        return copies
+
+    def column_step(step, carry):
+        span = pl.ds(pl.multiple_of(step * block, block), block)
+        value = jnp.dot(active, downs[:, span], preferred_element_type=jnp.float32)
+        result[:, span] = value.astype(jnp.bfloat16)
+        for copy in out_copies(step):
+            copy.start()
+        return carry
+
+    def finish_step(step, carry):
+        for copy in out_copies(step):
+            copy.wait()
+        return carry
+
+    lax.fori_loop(0, column_blocks, column_step, 0)
+    lax.fori_loop(0, column_blocks, finish_step, 0)
+
+
+def experts_of(pieces, out_rows, gate_weight, up_weight, down_weight, top):
+    local_experts, shard_units, model_width = gate_weight.shape
+    units = local_experts * shard_units
+    unit_block = 256 if units % 256 == 0 else 128
+    block = 512
+    pieces_in = [piece.shape[0] for piece in pieces]
+    total = sum(pieces_in)
+    packed = pieces[0].shape[1]
+    own = jnp.full((1,), lax.axis_index("exp") * local_experts, jnp.int32)
+    anywhere = pl.BlockSpec(memory_space=pl.ANY)
+    kernel = functools.partial(
+        expert_kernel, pieces_in, out_rows, local_experts, shard_units, model_width, top, block
+    )
+    return pl.pallas_call(
+        kernel,
+        out_shape=[jax.ShapeDtypeStruct((count, model_width), jnp.bfloat16) for count in out_rows],
+        in_specs=[pl.BlockSpec(memory_space=pltpu.SMEM)] + [anywhere] * (len(pieces) + 3),
+        out_specs=[anywhere] * len(out_rows),
+        scratch_shapes=[
+            pltpu.VMEM((total, packed), jnp.bfloat16),
+            pltpu.VMEM((units // unit_block, unit_block, model_width), jnp.bfloat16),
+            pltpu.VMEM((units // unit_block, unit_block, model_width), jnp.bfloat16),
+            pltpu.VMEM((units, model_width), jnp.bfloat16),
+            pltpu.VMEM((units // unit_block, total, unit_block), jnp.bfloat16),
+            pltpu.VMEM((total, model_width), jnp.bfloat16),
+            pltpu.SemaphoreType.DMA((len(pieces),)),
+            pltpu.SemaphoreType.DMA((units // unit_block,)),
+            pltpu.SemaphoreType.DMA((units // unit_block,)),
+            pltpu.SemaphoreType.DMA,
+            pltpu.SemaphoreType.DMA((model_width // block, len(out_rows))),
+        ],
+        compiler_params=pltpu.CompilerParams(vmem_limit_bytes=48 * 1024 * 1024),
+        cost_estimate=pl.CostEstimate(
+            flops=6 * total * units * model_width,
+            bytes_accessed=6 * units * model_width + 4 * total * model_width,
+            transcendentals=total * units,
+        ),
+        name="experts",
+    )(
+        own,
+        *pieces,
+        gate_weight.reshape(units, model_width),
+        up_weight.reshape(units, model_width),
+        down_weight.reshape(units, model_width),
+    )
+
+
+def with_routing(tokens, routed_experts, route_weights):
+    high = route_weights.astype(jnp.bfloat16)
+    low = (route_weights - high.astype(jnp.float32)).astype(jnp.bfloat16)
+    extra = jnp.concatenate([routed_experts.astype(jnp.bfloat16), high, low], axis=1)
+    extra = jnp.pad(extra, ((0, 0), (0, 128 - extra.shape[1])))
+    return jnp.concatenate([tokens, extra], axis=1)
+
+
+def on_device_dense(tokens, routed_experts, route_weights, gate_weight, up_weight, down_weight):
+    top = routed_experts.shape[1]
+    packed = with_routing(tokens, routed_experts, route_weights)
+    rows = lax.all_gather(packed, ("rep", "exp"), axis=0, tiled=True)
+    partial = experts_of([rows], [rows.shape[0]], gate_weight, up_weight, down_weight, top)[0]
+    return lax.psum_scatter(partial, ("rep", "exp"), scatter_dimension=0, tiled=True)
+
+
 def solution(mesh):
     placed = (
         P(("rep", "exp"), None),
@@ -87,6 +247,11 @@
         P("exp", "rep", None),
         P("exp", "rep", None),
     )
+    plane = mesh.shape["exp"] == 8 and mesh.shape["rep"] == 4
     return jax.shard_map(
-        on_device, mesh=mesh, in_specs=placed, out_specs=P(("rep", "exp"), None), check_vma=False
-    )
+        on_device_dense if plane else on_device_slots,
+        mesh=mesh,
+        in_specs=placed,
+        out_specs=P(("rep", "exp"), None),
+        check_vma=False,
+    )

time: 336 us -> 242 us (0.72)
  blocking collectives: 52.4 us -> 0 us
  local copies, waits for them, and re-layouts: 50.6 us -> 2.86 us
  matrix products: 22.3 us -> 0 us
  waiting for transfers between devices: 183 us -> 205 us
  Pallas kernels: 0 us -> 18.1 us
  other arithmetic: 9.43 us -> 3.04 us
  starting transfers between devices: 4.91 us -> 0.04 us
    reduce_scatter x1, waiting for transfers between devices: 23.7 us -> 139 us  [on_device_dense(): lax.psum_scatter(partial, ('rep', 'exp'), scatter_dimension=0, tiled=True)]
    all_gather x1, waiting for transfers between devices: 115 us -> 65.3 us  [on_device_dense(): rows = lax.all_gather(packed, ('rep', 'exp'), axis=0, tiled=True)]
    all_to_all x1 -> x0, waiting for transfers between devices: 44 us -> none  [on_device(): lax.all_to_all(outcomes, 'exp', split_axis=2, concat_axis=0, tiled=True)]
    all_gather x2 -> x0, blocking collectives: 26.4 us -> none  [the longest x1 13.3 us: routing_column(): lax.all_gather(route_weights, 'rep', axis=0, tiled=True)]
    all_to_all x1 -> x0, blocking collectives: 25.9 us -> none  [on_device(): lax.all_to_all(buffer, 'exp', split_axis=0, concat_axis=2, tiled=True)]
    dot_general x3 -> x0, matrix products: 22.3 us -> none  [the longest x1 12.4 us: on_device(): jnp.einsum('emf,efd->emd', hidden, down_weight, preferred_element_type=jn...]
    pallas_call x0 -> x1, Pallas kernels: none -> 18.1 us  [experts_of(): pl.pallas_call(kernel, out_shape=[jax.ShapeDtypeStruct((count, model_widt...]
    gather x1 -> x0, local copies, waits for them, and re-layouts: 14.3 us -> none  [on_device(): returned[expert_index, replica_index, place_index].astype(jnp.float32)]
  transfers between devices with their start and end apart: 3 -> 2, of which waited for: 3 -> 2; matrix products, arithmetic and copies ran while one was open for 0% -> 0% of each run, Pallas kernels for 0% -> 0%
where the time goes in v2:
time: 242 us
  waiting for transfers between devices  205 us (85%)
  Pallas kernels  18.1 us (7%)
  between operations  13.4 us (6%)
  other arithmetic  3.04 us (1%)
  local copies, waits for them, and re-layouts  2.86 us (1%)
    reduce_scatter x1, waiting for transfers between devices, on_device_dense(): lax.psum_scatter(partial, ('rep', 'exp'), scatter_dimension=0, tiled=True)  139 us
    all_gather x1, waiting for transfers between devices, on_device_dense(): rows = lax.all_gather(packed, ('rep', 'exp'), axis=0, tiled=True)  65.3 us
    pallas_call x1, Pallas kernels, experts_of(): pl.pallas_call(kernel, out_shape=[jax.ShapeDtypeStruct((count, model_widt...  18.1 us
  transfers between devices with their start and end apart: 2, of which 2 were waited for; matrix products, arithmetic and copies ran while one was open for 0% of the time, Pallas kernels for 0%

profile of v2, /device:TPU:0, one launch (start us, length us, event | category | flops | bytes accessed | tf_op | source)
XLA Modules:
  0.0 242.3 jit_solution(9091514653810159418)
XLA Ops:
  6.5 0.0 all-gather.2.cloned.1.call-start
  6.5 0.7 convert_element_type.15
  7.2 0.8 copy.11
  8.0 0.7 convert_element_type.14
  8.7 0.1 copy.12
  8.8 0.1 copy.13
  8.9 0.1 fusion.4
  8.9 1.6 pad_maximum_fusion
  10.5 0.0 all-gather.2.cloned.1.call-update
  10.5 0.0 reduce-scatter.2.cloned.1.call-start
  10.6 65.3 %all-gather.2.cloned.1.call-done.refs_1_ = bf16[512,4224]{1,0:T(8,128)(2,1)} async-done(((bf16[16,4224]{1,0:T(8,128)(2,1)}), bf16[512,4224]{1,0:T(8,128)(2,1)}) %all-gather.2.cloned.1.call-update) | async-done | bytes 4325392 | tf_op jit(solution)/shard_map/all_gather | solution.py:236
  75.9 18.1 %experts.1 = bf16[512,4096]{1,0:T(8,128)(2,1)S(1)} custom-call(s32[1]{0:T(128)} %bitcast.refs_0_, bf16[512,4224]{1,0:T(8,128)(2,1)} %all-gather.2.cloned.1.call-done.refs_1_, bf16[768,4096]{1,0:T(8,128)(2,1)} %bitcast.4, bf16[768,4096]{1,0:T(8,128)(2,1)} %bitcast.5, bf16[768,4096]{1,0:T(8,128)(2,1)} %bitcast.6), custom_call_target="tpu_custom_call" | custom-call | flops 9663676416 | bytes 27262976 | tf_op jit(solution)/shard_map/experts/pallas_call | solution.py:191
  94.0 0.0 copy-start
  94.0 1.9 copy-done
  96.0 0.0 reduce-scatter.2.cloned.1.call-update
  96.0 139.4 %reduce-scatter.2.cloned.1.call-done = bf16[16,4096]{1,0:T(8,128)(2,1)} async-done(((bf16[512,4096]{1,0:T(8,128)(2,1)}), bf16[16,4096]{1,0:T(8,128)(2,1)}) %reduce-scatter.2.cloned.1.call-update) | async-done | bytes 131088 | tf_op jit(solution)/shard_map/reduce_scatter | solution.py:238
  (1 shorter events, 0.0 us)
Async XLA Ops:
  6.5 69.4 %all-gather.2.cloned.1.call-start = ((), (), s32[]{:S(2)}) async-start(), calls=%async_computation.1 | async-start | bytes 4460544 | tf_op jit(solution)/shard_map/all_gather | solution.py:236
  10.5 224.9 %reduce-scatter.2.cloned.1.call-start = ((), (), s32[]{:S(2)}) async-start(), calls=%async_computation.2 | async-start | bytes 4325376 | tf_op jit(solution)/shard_map/reduce_scatter | solution.py:238
  94.0 1.9 copy-start
Sparse Core Ops, SparseCore 0:
  10.6 65.2 all-gather.1
  96.1 139.2 reduce-scatter.1

commit v3 on v2

--- a/solution.py
+++ b/solution.py
@@ -109,13 +109,15 @@
 
     for copy in row_copies:
         copy.start()
-    for step in range(unit_blocks):
+    for copy in weight_copies(0):
+        copy.start()
+    for copy in row_copies:
+        copy.wait()
+    for step in range(1, unit_blocks):
         for copy in weight_copies(step):
             copy.start()
     down_copy = pltpu.make_async_copy(down_hbm, downs, down_sem)
     down_copy.start()
-    for copy in row_copies:
-        copy.wait()
 
     extra = rows[:, model_width:].astype(jnp.float32)
     width = extra.shape[1]
@@ -222,6 +224,20 @@
     )
 
 
+def swap_exp(value, bit):
+    owners = lax.axis_size("exp")
+    return lax.ppermute(value, "exp", [(i, i ^ bit) for i in range(owners)])
+
+
+def turn_rep(value, shift):
+    replicas = lax.axis_size("rep")
+    return lax.ppermute(value, "rep", [(i, (i - shift) % replicas) for i in range(replicas)])
+
+
+def add(left, right):
+    return (left.astype(jnp.float32) + right.astype(jnp.float32)).astype(jnp.bfloat16)
+
+
 def with_routing(tokens, routed_experts, route_weights):
     high = route_weights.astype(jnp.bfloat16)
     low = (route_weights - high.astype(jnp.float32)).astype(jnp.bfloat16)
@@ -231,11 +247,35 @@
 
 
 def on_device_dense(tokens, routed_experts, route_weights, gate_weight, up_weight, down_weight):
+    replicas = lax.axis_size("rep")
+    token_rows = tokens.shape[0]
+    half = replicas // 2
     top = routed_experts.shape[1]
     packed = with_routing(tokens, routed_experts, route_weights)
-    rows = lax.all_gather(packed, ("rep", "exp"), axis=0, tiled=True)
-    partial = experts_of([rows], [rows.shape[0]], gate_weight, up_weight, down_weight, top)[0]
-    return lax.psum_scatter(partial, ("rep", "exp"), scatter_dimension=0, tiled=True)
+    blocks = [packed] + [turn_rep(packed, s) for s in range(1, replicas)]
+    first = jnp.concatenate(blocks[:half], axis=0)
+    second = jnp.concatenate(blocks[half:], axis=0)
+    first = jnp.concatenate([first, swap_exp(first, 2)], axis=0)
+    second = jnp.concatenate([second, swap_exp(second, 4)], axis=0)
+    planes = [first, swap_exp(first, 4), second, swap_exp(second, 2)]
+    planes = planes + [swap_exp(plane, 1) for plane in planes]
+
+    cuts = [plane.shape[0] for plane in planes]
+    parts = experts_of(planes, cuts, gate_weight, up_weight, down_weight, top)
+    returned = [swap_exp(part, 1) for part in parts[4:]]
+    first_away, second_away = add(parts[1], returned[1]), add(parts[3], returned[3])
+    first_back, second_back = swap_exp(first_away, 4), swap_exp(second_away, 2)
+    first = add(add(parts[0], returned[0]), first_back)
+    second = add(add(parts[2], returned[2]), second_back)
+    size = first.shape[0] // 2
+    first_back, second_back = swap_exp(first[size:], 2), swap_exp(second[size:], 4)
+    first, second = add(first[:size], first_back), add(second[:size], second_back)
+    column = [*jnp.split(first, half, axis=0), *jnp.split(second, replicas - half, axis=0)]
+    arrived = [turn_rep(column[s], -s) for s in range(1, replicas)]
+    total = column[0].astype(jnp.float32)
+    for part in arrived:
+        total = total + part.astype(jnp.float32)
+    return total.astype(jnp.bfloat16)
 
 
 def solution(mesh):

time: 242 us -> 98.2 us (0.41)
  waiting for transfers between devices: 205 us -> 49.1 us
  starting transfers between devices: 0.04 us -> 26 us
  between operations: 13.4 us -> 0.14 us
    reduce_scatter x1 -> x0, waiting for transfers between devices: 139 us -> none  [on_device_dense(): lax.psum_scatter(partial, ('rep', 'exp'), scatter_dimension=0, tiled=True)]
    all_gather x1 -> x0, waiting for transfers between devices: 65.3 us -> none  [on_device_dense(): rows = lax.all_gather(packed, ('rep', 'exp'), axis=0, tiled=True)]
    ppermute x0 -> x22, waiting for transfers between devices: none -> 49.1 us  [the longest x16 36.1 us: swap_exp(): return lax.ppermute(value, 'exp', [(i, i ^ bit) for i in range(owners)])]
    ppermute x0 -> x22, starting transfers between devices: none -> 26 us  [the longest x6 14.1 us: turn_rep(): lax.ppermute(value, 'rep', [(i, (i - shift) % replicas) for i in range(re...]
  transfers between devices with their start and end apart: 2 -> 22, of which waited for: 2 -> 15; matrix products, arithmetic and copies ran while one was open for 0% -> 2% of each run, Pallas kernels for 0% -> 0%
where the time goes in v3:
time: 98.2 us; the launch traced here: 97.9 us
  waiting for transfers between devices  49.1 us (50%)
  starting transfers between devices  26 us (26%)
  Pallas kernels  16.8 us (17%)
  other arithmetic  4.85 us (5%)
  local copies, waits for them, and re-layouts  1.06 us (1%)
    ppermute x16, waiting for transfers between devices, swap_exp(): return lax.ppermute(value, 'exp', [(i, i ^ bit) for i in range(owners)])  36.1 us
    pallas_call x1, Pallas kernels, experts_of(): pl.pallas_call(kernel, out_shape=[jax.ShapeDtypeStruct((count, model_widt...  16.8 us
    ppermute x6, starting transfers between devices, turn_rep(): lax.ppermute(value, 'rep', [(i, (i - shift) % replicas) for i in range(re...  14.1 us
    ppermute x6, waiting for transfers between devices, turn_rep(): lax.ppermute(value, 'rep', [(i, (i - shift) % replicas) for i in range(re...  13 us
    ppermute x16, starting transfers between devices, swap_exp(): return lax.ppermute(value, 'exp', [(i, i ^ bit) for i in range(owners)])  11.9 us
  transfers between devices with their start and end apart: 22, of which 15 were waited for; matrix products, arithmetic and copies ran while one was open for 2% of the time, Pallas kernels for 0%

profile of v3, /device:TPU:0, one launch (start us, length us, event | category | flops | bytes accessed | tf_op | source)
XLA Modules:
  0.0 97.9 jit_solution(17252619047839662121)
XLA Ops:
  0.0 0.7 convert_element_type.102
  0.7 0.8 copy.11
  1.4 0.7 convert_element_type.101
  2.4 0.9 pad_maximum_fusion.3
  3.3 3.1 %collective-permute-start.4 = (bf16[16,4224]{1,0:T(8,128)(2,1)S(1)}, bf16[16,4224]{1,0:T(8,128)(2,1)S(1)}, u32[]{:S(2)}, u32[]{:S(2)}) collective-permute-start(bf16[16,4224]{1,0:T(8,128)(2,1)S(1)} %pad_maximum_fusion.3), channel_id=1, source_target_pairs={{0,8},{8,16},{16,24},{24,0},{1,9},{9,17},{17,25},{25,1},{2,10},{10... | collective-permute-start | bytes 405512 | tf_op jit(solution)/shard_map/ppermute | solution.py:234
  6.4 2.6 %collective-permute-start.3 = (bf16[16,4224]{1,0:T(8,128)(2,1)S(1)}, bf16[16,4224]{1,0:T(8,128)(2,1)S(1)}, u32[]{:S(2)}, u32[]{:S(2)}) collective-permute-start(bf16[16,4224]{1,0:T(8,128)(2,1)S(1)} %pad_maximum_fusion.3), channel_id=1, source_target_pairs={{0,16},{8,24},{16,0},{24,8},{1,17},{9,25},{17,1},{25,9},{2,18},{10... | collective-permute-start | bytes 405512 | tf_op jit(solution)/shard_map/ppermute | solution.py:234
  9.0 1.3 %collective-permute-start = (bf16[16,4224]{1,0:T(8,128)(2,1)S(1)}, bf16[16,4224]{1,0:T(8,128)(2,1)S(1)}, u32[]{:S(2)}, u32[]{:S(2)}) collective-permute-start(bf16[16,4224]{1,0:T(8,128)(2,1)S(1)} %pad_maximum_fusion.3), channel_id=1, source_target_pairs={{0,24},{8,0},{16,8},{24,16},{1,25},{9,1},{17,9},{25,17},{2,26},{10... | collective-permute-start | bytes 405512 | tf_op jit(solution)/shard_map/ppermute | solution.py:234
  10.3 2.6 %collective-permute-done.4 = bf16[16,4224]{1,0:T(8,128)(2,1)S(1)} collective-permute-done((bf16[16,4224]{1,0:T(8,128)(2,1)S(1)}, bf16[16,4224]{1,0:T(8,128)(2,1)S(1)}, u32[]{:S(2)}, u32[]{:S(2)}) %collective-permute-start.4) | collective-permute-done | bytes 135200 | tf_op jit(solution)/shard_map/ppermute | solution.py:234
  12.9 5.0 %collective-permute-done.3 = bf16[16,4224]{1,0:T(8,128)(2,1)S(1)} collective-permute-done((bf16[16,4224]{1,0:T(8,128)(2,1)S(1)}, bf16[16,4224]{1,0:T(8,128)(2,1)S(1)}, u32[]{:S(2)}, u32[]{:S(2)}) %collective-permute-start.3) | collective-permute-done | bytes 135200 | tf_op jit(solution)/shard_map/ppermute | solution.py:234
  17.9 1.6 %collective-permute-start.5 = (bf16[32,4224]{1,0:T(8,128)(2,1)S(1)}, bf16[32,4224]{1,0:T(8,128)(2,1)S(1)}, u32[]{:S(2)}, u32[]{:S(2)}) collective-permute-start(bf16[32,4224]{1,0:T(8,128)(2,1)S(1)} %pad_maximum_fusion.2), channel_id=1, source_target_pairs={{0,4},{1,5},{2,6},{3,7},{4,0},{5,1},{6,2},{7,3},{8,12},{9,13},{10,... | collective-permute-start | bytes 811016 | tf_op jit(solution)/shard_map/ppermute | solution.py:229
  19.5 0.9 pad_maximum_fusion.1
  20.4 1.6 %collective-permute-start.1 = (bf16[32,4224]{1,0:T(8,128)(2,1)S(1)}, bf16[32,4224]{1,0:T(8,128)(2,1)S(1)}, u32[]{:S(2)}, u32[]{:S(2)}) collective-permute-start(bf16[32,4224]{1,0:T(8,128)(2,1)S(1)} %pad_maximum_fusion.1), channel_id=1, source_target_pairs={{0,2},{1,3},{2,0},{3,1},{4,6},{5,7},{6,4},{7,5},{8,10},{9,11},{10,... | collective-permute-start | bytes 811016 | tf_op jit(solution)/shard_map/ppermute | solution.py:229
  22.0 4.3 %collective-permute-done.5 = bf16[32,4224]{1,0:T(8,128)(2,1)S(1)} collective-permute-done((bf16[32,4224]{1,0:T(8,128)(2,1)S(1)}, bf16[32,4224]{1,0:T(8,128)(2,1)S(1)}, u32[]{:S(2)}, u32[]{:S(2)}) %collective-permute-start.5) | collective-permute-done | bytes 270368 | tf_op jit(solution)/shard_map/ppermute | solution.py:229
  26.3 1.6 %collective-permute-start.6 = (bf16[64,4224]{1,0:T(8,128)(2,1)S(1)}, bf16[64,4224]{1,0:T(8,128)(2,1)S(1)}, u32[]{:S(2)}, u32[]{:S(2)}) collective-permute-start(bf16[64,4224]{1,0:T(8,128)(2,1)S(1)} %constant_dynamic-update-slice_fusion.refs_3_), channel_id=1, source_target_pairs={{0,2},{1,3},{2,0},{3,1},{4,6},{5,7},{6,4},{7,5},{8,10},{9,11},{10,... | collective-permute-start | bytes 1622024 | tf_op jit(solution)/shard_map/ppermute | solution.py:229
  27.9 1.1 %collective-permute-done.1 = bf16[32,4224]{1,0:T(8,128)(2,1)S(1)} collective-permute-done((bf16[32,4224]{1,0:T(8,128)(2,1)S(1)}, bf16[32,4224]{1,0:T(8,128)(2,1)S(1)}, u32[]{:S(2)}, u32[]{:S(2)}) %collective-permute-start.1) | collective-permute-done | bytes 270368 | tf_op jit(solution)/shard_map/ppermute | solution.py:229
  30.0 10.1 %collective-permute-done.6.refs_4_ = bf16[64,4224]{1,0:T(8,128)(2,1)S(1)} collective-permute-done((bf16[64,4224]{1,0:T(8,128)(2,1)S(1)}, bf16[64,4224]{1,0:T(8,128)(2,1)S(1)}, u32[]{:S(2)}, u32[]{:S(2)}) %collective-permute-start.6) | collective-permute-done | bytes 540704 | tf_op jit(solution)/shard_map/ppermute | solution.py:229
  40.1 1.4 %collective-permute-done.2.refs_2_ = bf16[64,4224]{1,0:T(8,128)(2,1)S(1)} collective-permute-done((bf16[64,4224]{1,0:T(8,128)(2,1)S(1)}, bf16[64,4224]{1,0:T(8,128)(2,1)S(1)}, u32[]{:S(2)}, u32[]{:S(2)}) %collective-permute-start.2) | collective-permute-done | bytes 540704 | tf_op jit(solution)/shard_map/ppermute | solution.py:229
  42.2 1.4 %collective-permute-done.8.refs_6_ = bf16[64,4224]{1,0:T(8,128)(2,1)} collective-permute-done((bf16[64,4224]{1,0:T(8,128)(2,1)S(1)}, bf16[64,4224]{1,0:T(8,128)(2,1)}, u32[]{:S(2)}, u32[]{:S(2)}) %collective-permute-start.8) | collective-permute-done | bytes 540704 | tf_op jit(solution)/shard_map/ppermute | solution.py:229
  43.7 16.8 %experts.1 = (bf16[64,4096]{1,0:T(8,128)(2,1)S(1)}, bf16[64,4096]{1,0:T(8,128)(2,1)S(1)}, bf16[64,4096]{1,0:T(8,128)(2,1)S(1)}, bf16[64,4096]{1,0:T(8,128)(2,1)S...) custom-call(s32[1]{0:T(128)} %bitcast.refs_0_, ...), custom_call_target="tpu_custom_call" | custom-call | flops 9663676416 | bytes 27262976 | tf_op jit(solution)/shard_map/experts/pallas_call | solution.py:193
  61.6 0.9 collective-permute-done.12
  62.6 1.0 collective-permute-start.13
  63.6 1.2 %collective-permute-done.17 = bf16[64,4096]{1,0:T(8,128)(2,1)S(1)} collective-permute-done((bf16[64,4096]{1,0:T(8,128)(2,1)S(1)}, bf16[64,4096]{1,0:T(8,128)(2,1)S(1)}, u32[]{:S(2)}, u32[]{:S(2)}) %collective-permute-start.17) | collective-permute-done | bytes 524320 | tf_op jit(solution)/shard_map/ppermute | solution.py:229
  64.8 1.6 %collective-permute-start.18 = (bf16[64,4096]{1,0:T(8,128)(2,1)S(1)}, bf16[64,4096]{1,0:T(8,128)(2,1)S(1)}, u32[]{:S(2)}, u32[]{:S(2)}) collective-permute-start(bf16[64,4096]{1,0:T(8,128)(2,1)S(1)} %add_convert_fusion.1), channel_id=1, source_target_pairs={{0,2},{1,3},{2,0},{3,1},{4,6},{5,7},{6,4},{7,5},{8,10},{9,11},{10,... | collective-permute-start | bytes 1572872 | tf_op jit(solution)/shard_map/ppermute | solution.py:229
  66.4 10.2 %collective-permute-done.13 = bf16[64,4096]{1,0:T(8,128)(2,1)S(1)} collective-permute-done((bf16[64,4096]{1,0:T(8,128)(2,1)S(1)}, bf16[64,4096]{1,0:T(8,128)(2,1)S(1)}, u32[]{:S(2)}, u32[]{:S(2)}) %collective-permute-start.13) | collective-permute-done | bytes 524320 | tf_op jit(solution)/shard_map/ppermute | solution.py:229
  76.8 1.6 %collective-permute-start.14 = (bf16[32,4096]{1,0:T(8,128)(2,1)S(1)}, bf16[32,4096]{1,0:T(8,128)(2,1)S(1)}, u32[]{:S(2)}, u32[]{:S(2)}) collective-permute-start(bf16[32,4096]{1,0:T(8,128)(2,1)S(1)} %slice.17), channel_id=1, source_target_pairs={{0,2},{1,3},{2,0},{3,1},{4,6},{5,7},{6,4},{7,5},{8,10},{9,11},{10,... | collective-permute-start | bytes 786440 | tf_op jit(solution)/shard_map/ppermute | solution.py:229
  79.1 1.0 collective-permute-start.19
  80.1 4.4 %collective-permute-done.14 = bf16[32,4096]{1,0:T(8,128)(2,1)S(1)} collective-permute-done((bf16[32,4096]{1,0:T(8,128)(2,1)S(1)}, bf16[32,4096]{1,0:T(8,128)(2,1)S(1)}, u32[]{:S(2)}, u32[]{:S(2)}) %collective-permute-start.14) | collective-permute-done | bytes 262176 | tf_op jit(solution)/shard_map/ppermute | solution.py:229
  84.6 2.6 %collective-permute-start.15 = (bf16[16,4096]{1,0:T(8,128)(2,1)S(1)}, bf16[16,4096]{1,0:T(8,128)(2,1)S(1)}, u32[]{:S(2)}, u32[]{:S(2)}) collective-permute-start(bf16[16,4096]{1,0:T(8,128)(2,1)S(1)} %split.17), channel_id=1, source_target_pairs={{0,8},{8,16},{16,24},{24,0},{1,9},{9,17},{17,25},{25,1},{2,10},{10... | collective-permute-start | bytes 393224 | tf_op jit(solution)/shard_map/ppermute | solution.py:234
  87.3 0.9 collective-permute-start.20
  88.1 3.6 %collective-permute-start.21 = (bf16[16,4096]{1,0:T(8,128)(2,1)S(1)}, bf16[16,4096]{1,0:T(8,128)(2,1)S(1)}, u32[]{:S(2)}, u32[]{:S(2)}) collective-permute-start(bf16[16,4096]{1,0:T(8,128)(2,1)S(1)} %get-tuple-element.22), channel_id=1, source_target_pairs={{0,24},{8,0},{16,8},{24,16},{1,25},{9,1},{17,9},{25,17},{2,26},{10... | collective-permute-start | bytes 393224 | tf_op jit(solution)/shard_map/ppermute | solution.py:234
  92.2 5.0 %collective-permute-done.20 = bf16[16,4096]{1,0:T(8,128)(2,1)S(1)} collective-permute-done((bf16[16,4096]{1,0:T(8,128)(2,1)S(1)}, bf16[16,4096]{1,0:T(8,128)(2,1)S(1)}, u32[]{:S(2)}, u32[]{:S(2)}) %collective-permute-start.20) | collective-permute-done | bytes 131104 | tf_op jit(solution)/shard_map/ppermute | solution.py:234
  97.2 0.7 add_convert_fusion.8
  (46 shorter events, 4.9 us)
Async XLA Ops:
  3.3 25.6 %copy-start = (bf16[16,4096]{1,0:T(8,128)(2,1)S(1)}, bf16[16,4096]{1,0:T(8,128)(2,1)}, u32[]{:S(2)}) copy-start(bf16[16,4096]{1,0:T(8,128)(2,1)} %param.6) | copy-start | bytes 393220
  3.3 9.6 %collective-permute-start.4 = (bf16[16,4224]{1,0:T(8,128)(2,1)S(1)}, bf16[16,4224]{1,0:T(8,128)(2,1)S(1)}, u32[]{:S(2)}, u32[]{:S(2)}) collective-permute-start(bf16[16,4224]{1,0:T(8,128)(2,1)S(1)} %pad_maximum_fusion.3), channel_id=1, source_target_pairs={{0,8},{8,16},{16,24},{24,0},{1,9},{9,17},{17,25},{25,1},{2,10},{10... | collective-permute-start | bytes 405512 | tf_op jit(solution)/shard_map/ppermute | solution.py:234
  6.4 11.5 %collective-permute-start.3 = (bf16[16,4224]{1,0:T(8,128)(2,1)S(1)}, bf16[16,4224]{1,0:T(8,128)(2,1)S(1)}, u32[]{:S(2)}, u32[]{:S(2)}) collective-permute-start(bf16[16,4224]{1,0:T(8,128)(2,1)S(1)} %pad_maximum_fusion.3), channel_id=1, source_target_pairs={{0,16},{8,24},{16,0},{24,8},{1,17},{9,25},{17,1},{25,9},{2,18},{10... | collective-permute-start | bytes 405512 | tf_op jit(solution)/shard_map/ppermute | solution.py:234
  9.0 10.5 %collective-permute-start = (bf16[16,4224]{1,0:T(8,128)(2,1)S(1)}, bf16[16,4224]{1,0:T(8,128)(2,1)S(1)}, u32[]{:S(2)}, u32[]{:S(2)}) collective-permute-start(bf16[16,4224]{1,0:T(8,128)(2,1)S(1)} %pad_maximum_fusion.3), channel_id=1, source_target_pairs={{0,24},{8,0},{16,8},{24,16},{1,25},{9,1},{17,9},{25,17},{2,26},{10... | collective-permute-start | bytes 405512 | tf_op jit(solution)/shard_map/ppermute | solution.py:234
  17.9 8.4 %collective-permute-start.5 = (bf16[32,4224]{1,0:T(8,128)(2,1)S(1)}, bf16[32,4224]{1,0:T(8,128)(2,1)S(1)}, u32[]{:S(2)}, u32[]{:S(2)}) collective-permute-start(bf16[32,4224]{1,0:T(8,128)(2,1)S(1)} %pad_maximum_fusion.2), channel_id=1, source_target_pairs={{0,4},{1,5},{2,6},{3,7},{4,0},{5,1},{6,2},{7,3},{8,12},{9,13},{10,... | collective-permute-start | bytes 811016 | tf_op jit(solution)/shard_map/ppermute | solution.py:229
  20.4 8.5 %collective-permute-start.1 = (bf16[32,4224]{1,0:T(8,128)(2,1)S(1)}, bf16[32,4224]{1,0:T(8,128)(2,1)S(1)}, u32[]{:S(2)}, u32[]{:S(2)}) collective-permute-start(bf16[32,4224]{1,0:T(8,128)(2,1)S(1)} %pad_maximum_fusion.1), channel_id=1, source_target_pairs={{0,2},{1,3},{2,0},{3,1},{4,6},{5,7},{6,4},{7,5},{8,10},{9,11},{10,... | collective-permute-start | bytes 811016 | tf_op jit(solution)/shard_map/ppermute | solution.py:229
  26.3 13.8 %collective-permute-start.6 = (bf16[64,4224]{1,0:T(8,128)(2,1)S(1)}, bf16[64,4224]{1,0:T(8,128)(2,1)S(1)}, u32[]{:S(2)}, u32[]{:S(2)}) collective-permute-start(bf16[64,4224]{1,0:T(8,128)(2,1)S(1)} %constant_dynamic-update-slice_fusion.refs_3_), channel_id=1, source_target_pairs={{0,2},{1,3},{2,0},{3,1},{4,6},{5,7},{6,4},{7,5},{8,10},{9,11},{10,... | collective-permute-start | bytes 1622024 | tf_op jit(solution)/shard_map/ppermute | solution.py:229
  29.0 12.6 %collective-permute-start.2 = (bf16[64,4224]{1,0:T(8,128)(2,1)S(1)}, bf16[64,4224]{1,0:T(8,128)(2,1)S(1)}, u32[]{:S(2)}, u32[]{:S(2)}) collective-permute-start(bf16[64,4224]{1,0:T(8,128)(2,1)S(1)} %pad_maximum_fusion.refs_1_), channel_id=1, source_target_pairs={{0,4},{1,5},{2,6},{3,7},{4,0},{5,1},{6,2},{7,3},{8,12},{9,13},{10,... | collective-permute-start | bytes 1622024 | tf_op jit(solution)/shard_map/ppermute | solution.py:229
  29.5 12.1 %collective-permute-start.9 = (bf16[64,4224]{1,0:T(8,128)(2,1)S(1)}, bf16[64,4224]{1,0:T(8,128)(2,1)S(1)}, u32[]{:S(2)}, u32[]{:S(2)}) collective-permute-start(bf16[64,4224]{1,0:T(8,128)(2,1)S(1)} %constant_dynamic-update-slice_fusion.refs_3_), channel_id=1, source_target_pairs={{0,1},{1,0},{2,3},{3,2},{4,5},{5,4},{6,7},{7,6},{8,9},{9,8},{10,11... | collective-permute-start | bytes 1622024 | tf_op jit(solution)/shard_map/ppermute | solution.py:229
  29.5 12.1 %collective-permute-start.7 = (bf16[64,4224]{1,0:T(8,128)(2,1)S(1)}, bf16[64,4224]{1,0:T(8,128)(2,1)S(1)}, u32[]{:S(2)}, u32[]{:S(2)}) collective-permute-start(bf16[64,4224]{1,0:T(8,128)(2,1)S(1)} %pad_maximum_fusion.refs_1_), channel_id=1, source_target_pairs={{0,1},{1,0},{2,3},{3,2},{4,5},{5,4},{6,7},{7,6},{8,9},{9,8},{10,11... | collective-permute-start | bytes 1622024 | tf_op jit(solution)/shard_map/ppermute | solution.py:229
  40.1 3.5 %copy-start.1 = (bf16[64,4224]{1,0:T(8,128)(2,1)}, bf16[64,4224]{1,0:T(8,128)(2,1)S(1)}, u32[]{:S(2)}) copy-start(bf16[64,4224]{1,0:T(8,128)(2,1)S(1)} %collective-permute-done.6.refs_4_) | copy-start | bytes 1622020
  40.1 2.1 %collective-permute-start.10 = (bf16[64,4224]{1,0:T(8,128)(2,1)S(1)}, bf16[64,4224]{1,0:T(8,128)(2,1)}, u32[]{:S(2)}, u32[]{:S(2)}) collective-permute-start(bf16[64,4224]{1,0:T(8,128)(2,1)S(1)} %collective-permute-done.6.refs_4_), channel_id=1, source_target_pairs={{0,1},{1,0},{2,3},{3,2},{4,5},{5,4},{6,7},{7,6},{8,9},{9,8},{10,11... | collective-permute-start | bytes 1622024 | tf_op jit(solution)/shard_map/ppermute | solution.py:229
  41.6 2.1 %collective-permute-start.8 = (bf16[64,4224]{1,0:T(8,128)(2,1)S(1)}, bf16[64,4224]{1,0:T(8,128)(2,1)}, u32[]{:S(2)}, u32[]{:S(2)}) collective-permute-start(bf16[64,4224]{1,0:T(8,128)(2,1)S(1)} %collective-permute-done.2.refs_2_), channel_id=1, source_target_pairs={{0,1},{1,0},{2,3},{3,2},{4,5},{5,4},{6,7},{7,6},{8,9},{9,8},{10,11... | collective-permute-start | bytes 1622024 | tf_op jit(solution)/shard_map/ppermute | solution.py:229
  41.6 2.1 %copy-start.2 = (bf16[64,4224]{1,0:T(8,128)(2,1)}, bf16[64,4224]{1,0:T(8,128)(2,1)S(1)}, u32[]{:S(2)}) copy-start(bf16[64,4224]{1,0:T(8,128)(2,1)S(1)} %collective-permute-done.9.refs_7_) | copy-start | bytes 1622020
  41.6 2.1 %copy-start.3 = (bf16[64,4224]{1,0:T(8,128)(2,1)}, bf16[64,4224]{1,0:T(8,128)(2,1)S(1)}, u32[]{:S(2)}) copy-start(bf16[64,4224]{1,0:T(8,128)(2,1)S(1)} %collective-permute-done.7.refs_5_) | copy-start | bytes 1622020
  60.5 2.0 %collective-permute-start.12 = (bf16[64,4096]{1,0:T(8,128)(2,1)S(1)}, bf16[64,4096]{1,0:T(8,128)(2,1)S(1)}, u32[]{:S(2)}, u32[]{:S(2)}) collective-permute-start(bf16[64,4096]{1,0:T(8,128)(2,1)S(1)} %get-tuple-element.16), channel_id=1, source_target_pairs={{0,1},{1,0},{2,3},{3,2},{4,5},{5,4},{6,7},{7,6},{8,9},{9,8},{10,11... | collective-permute-start | bytes 1572872 | tf_op jit(solution)/shard_map/ppermute | solution.py:229
  60.7 5.7 %collective-permute-start.11 = (bf16[64,4096]{1,0:T(8,128)(2,1)S(1)}, bf16[64,4096]{1,0:T(8,128)(2,1)S(1)}, u32[]{:S(2)}, u32[]{:S(2)}) collective-permute-start(bf16[64,4096]{1,0:T(8,128)(2,1)S(1)} %get-tuple-element.14), channel_id=1, source_target_pairs={{0,1},{1,0},{2,3},{3,2},{4,5},{5,4},{6,7},{7,6},{8,9},{9,8},{10,11... | collective-permute-start | bytes 1572872 | tf_op jit(solution)/shard_map/ppermute | solution.py:229
  61.1 17.3 %collective-permute-start.16 = (bf16[64,4096]{1,0:T(8,128)(2,1)S(1)}, bf16[64,4096]{1,0:T(8,128)(2,1)S(1)}, u32[]{:S(2)}, u32[]{:S(2)}) collective-permute-start(bf16[64,4096]{1,0:T(8,128)(2,1)S(1)} %get-tuple-element.18), channel_id=1, source_target_pairs={{0,1},{1,0},{2,3},{3,2},{4,5},{5,4},{6,7},{7,6},{8,9},{9,8},{10,11... | collective-permute-start | bytes 1572872 | tf_op jit(solution)/shard_map/ppermute | solution.py:229
  61.2 3.5 %collective-permute-start.17 = (bf16[64,4096]{1,0:T(8,128)(2,1)S(1)}, bf16[64,4096]{1,0:T(8,128)(2,1)S(1)}, u32[]{:S(2)}, u32[]{:S(2)}) collective-permute-start(bf16[64,4096]{1,0:T(8,128)(2,1)S(1)} %get-tuple-element.20), channel_id=1, source_target_pairs={{0,1},{1,0},{2,3},{3,2},{4,5},{5,4},{6,7},{7,6},{8,9},{9,8},{10,11... | collective-permute-start | bytes 1572872 | tf_op jit(solution)/shard_map/ppermute | solution.py:229
  62.6 14.0 %collective-permute-start.13 = (bf16[64,4096]{1,0:T(8,128)(2,1)S(1)}, bf16[64,4096]{1,0:T(8,128)(2,1)S(1)}, u32[]{:S(2)}, u32[]{:S(2)}) collective-permute-start(bf16[64,4096]{1,0:T(8,128)(2,1)S(1)} %add_convert_fusion.4), channel_id=1, source_target_pairs={{0,4},{1,5},{2,6},{3,7},{4,0},{5,1},{6,2},{7,3},{8,12},{9,13},{10,... | collective-permute-start | bytes 1572872 | tf_op jit(solution)/shard_map/ppermute | solution.py:229
  64.8 14.0 %collective-permute-start.18 = (bf16[64,4096]{1,0:T(8,128)(2,1)S(1)}, bf16[64,4096]{1,0:T(8,128)(2,1)S(1)}, u32[]{:S(2)}, u32[]{:S(2)}) collective-permute-start(bf16[64,4096]{1,0:T(8,128)(2,1)S(1)} %add_convert_fusion.1), channel_id=1, source_target_pairs={{0,2},{1,3},{2,0},{3,1},{4,6},{5,7},{6,4},{7,5},{8,10},{9,11},{10,... | collective-permute-start | bytes 1572872 | tf_op jit(solution)/shard_map/ppermute | solution.py:229
  76.8 7.6 %collective-permute-start.14 = (bf16[32,4096]{1,0:T(8,128)(2,1)S(1)}, bf16[32,4096]{1,0:T(8,128)(2,1)S(1)}, u32[]{:S(2)}, u32[]{:S(2)}) collective-permute-start(bf16[32,4096]{1,0:T(8,128)(2,1)S(1)} %slice.17), channel_id=1, source_target_pairs={{0,2},{1,3},{2,0},{3,1},{4,6},{5,7},{6,4},{7,5},{8,10},{9,11},{10,... | collective-permute-start | bytes 786440 | tf_op jit(solution)/shard_map/ppermute | solution.py:229
  79.1 8.1 %collective-permute-start.19 = (bf16[32,4096]{1,0:T(8,128)(2,1)S(1)}, bf16[32,4096]{1,0:T(8,128)(2,1)S(1)}, u32[]{:S(2)}, u32[]{:S(2)}) collective-permute-start(bf16[32,4096]{1,0:T(8,128)(2,1)S(1)} %slice.19), channel_id=1, source_target_pairs={{0,4},{1,5},{2,6},{3,7},{4,0},{5,1},{6,2},{7,3},{8,12},{9,13},{10,... | collective-permute-start | bytes 786440 | tf_op jit(solution)/shard_map/ppermute | solution.py:229
  84.6 7.7 %collective-permute-start.15 = (bf16[16,4096]{1,0:T(8,128)(2,1)S(1)}, bf16[16,4096]{1,0:T(8,128)(2,1)S(1)}, u32[]{:S(2)}, u32[]{:S(2)}) collective-permute-start(bf16[16,4096]{1,0:T(8,128)(2,1)S(1)} %split.17), channel_id=1, source_target_pairs={{0,8},{8,16},{16,24},{24,0},{1,9},{9,17},{17,25},{25,1},{2,10},{10... | collective-permute-start | bytes 393224 | tf_op jit(solution)/shard_map/ppermute | solution.py:234
  87.3 9.9 %collective-permute-start.20 = (bf16[16,4096]{1,0:T(8,128)(2,1)S(1)}, bf16[16,4096]{1,0:T(8,128)(2,1)S(1)}, u32[]{:S(2)}, u32[]{:S(2)}) collective-permute-start(bf16[16,4096]{1,0:T(8,128)(2,1)S(1)} %get-tuple-element.21), channel_id=1, source_target_pairs={{0,16},{8,24},{16,0},{24,8},{1,17},{9,25},{17,1},{25,9},{2,18},{10... | collective-permute-start | bytes 393224 | tf_op jit(solution)/shard_map/ppermute | solution.py:234
  88.1 9.0 %collective-permute-start.21 = (bf16[16,4096]{1,0:T(8,128)(2,1)S(1)}, bf16[16,4096]{1,0:T(8,128)(2,1)S(1)}, u32[]{:S(2)}, u32[]{:S(2)}) collective-permute-start(bf16[16,4096]{1,0:T(8,128)(2,1)S(1)} %get-tuple-element.22), channel_id=1, source_target_pairs={{0,24},{8,0},{16,8},{24,16},{1,25},{9,1},{17,9},{25,17},{2,26},{10... | collective-permute-start | bytes 393224 | tf_op jit(solution)/shard_map/ppermute | solution.py:234
